TPU v7x, 32 devices: a whole 2x2x4 slice. The times are simulated.
32 devices in a mesh: section: 2 (over core), expert: 4 (over z), tensor: 4 (over y, x).
Axes of the slice: x: 2, y: 2, z: 4, core: 2. Of those that a mesh axis runs over, the one named last changes fastest.
Arguments:
- inputs: bfloat16 [2, 512, 768], P(None, 'expert'), may hold values from -6 to 6
- cotangent: bfloat16 [2, 512, 768], P(None, 'expert'), may hold values from -6 to 6
- attn_gain: bfloat16 [2, 768], P('section', 'expert'), may hold values from 0.5 to 1.5
- query_weight: bfloat16 [2, 768, 768], P('section', 'expert', 'tensor'), may hold values from -0.21875 to 0.21875
- key_weight: bfloat16 [2, 768, 768], P('section', 'expert', 'tensor'), may hold values from -0.21875 to 0.21875
- value_weight: bfloat16 [2, 768, 768], P('section', 'expert', 'tensor'), may hold values from -0.21875 to 0.21875
- out_weight: bfloat16 [2, 768, 768], P('section', 'expert', 'tensor'), may hold values from -1.75 to 1.75
- rel_table: bfloat16 [2, 32, 12], P('section', 'expert', 'tensor'), may hold values from -4 to 4
- ffn_gain: bfloat16 [2, 768], P('section', 'expert'), may hold values from 0.5 to 1.5
- router_weight: bfloat16 [2, 768, 4], P('section', 'expert'), may hold values from -0.15625 to 0.15625
- expert_in: bfloat16 [2, 4, 768, 3072], P('section', 'expert', None, 'tensor'), may hold values from -0.21875 to 0.21875
- expert_out: bfloat16 [2, 4, 3072, 768], P('section', 'expert', 'tensor'), may hold values from -0.625 to 0.625
- routes: int32 [2, 2, 512, 1], P('section', None, 'expert'), may hold values from 0 to 3; in each aligned block of 128 rows (0 to 127, 128 to 255, ..., all dimensions but the last counted through in order) at most 40 rows name the same one
- segments: int32 [2, 512], P(None, 'expert'), may hold values from 0 to 15, never falling along the last dimension, each value on 1 to 64 neighbouring positions
Outputs:
- section_outputs: bfloat16 [2, 2, 512, 768], P('section', None, 'expert')
- input_grads: bfloat16 [2, 2, 512, 768], P('section', None, 'expert')
- grad_attn_gain: float32 [2, 768], P('section', 'expert')
- grad_query_weight: float32 [2, 768, 768], P('section', 'expert', 'tensor')
- grad_key_weight: float32 [2, 768, 768], P('section', 'expert', 'tensor')
- grad_value_weight: float32 [2, 768, 768], P('section', 'expert', 'tensor')
- grad_out_weight: float32 [2, 768, 768], P('section', 'expert', 'tensor')
- grad_rel_table: float32 [2, 32, 12], P('section', 'expert', 'tensor')
- grad_ffn_gain: float32 [2, 768], P('section', 'expert')
- grad_router_weight: float32 [2, 768, 4], P('section', 'expert')
- grad_expert_in: float32 [2, 4, 768, 3072], P('section', 'expert', None, 'tensor')
- grad_expert_out: float32 [2, 4, 3072, 768], P('section', 'expert', 'tensor')
Inputs may be any that keep to these rules, and one draw needn't show every extreme that they name: `routes`: in each aligned block of 128 rows (one sequence of one micro-batch and layer) no expert is named by more than 40 rows, a bound that some block reaches. `segments`: document numbers never fall along the tokens; a document holds at most 64 tokens, and one holds exactly that many.
All inputs are finite; a program needn't handle non-finite values.
Results may differ from a plain program's by a relative error of at most 0.035.
Values may be sent and summed in bfloat16 or wider, within the bound.
A program may use at most 128 MiB of HBM per device.

v0:
```python
import math

import jax
import jax.numpy as jnp
from jax import lax
from jax.experimental import pallas as pl
from jax.experimental.pallas import tpu as pltpu
from jax.sharding import PartitionSpec as P

BUCKETS = 32


PEERS = 4
MESH = pl.DeviceIdType.MESH


def use_kernels():
    return (
        lax.axis_size("expert") == PEERS
        and lax.axis_size("tensor") == PEERS
        and lax.axis_size("section") == 2
    )


def around(axis, distance):
    return lax.rem(lax.axis_index(axis) + distance, PEERS)


def greet(axes, sibling=False):
    barrier = pltpu.get_barrier_semaphore()
    count = 0
    for axis in axes:
        for distance in range(1, PEERS):
            pl.semaphore_signal(
                barrier, inc=1, device_id={axis: around(axis, distance)}, device_id_type=MESH
            )
            count += 1
    if sibling:
        pl.semaphore_signal(
            barrier,
            inc=1,
            device_id={"section": 1 - lax.axis_index("section")},
            device_id_type=MESH,
        )
        count += 1
    pl.semaphore_wait(barrier, count)


def send(source, target, sends, receives, slot, axis, peer):
    copy = pltpu.make_async_remote_copy(
        src_ref=source,
        dst_ref=target,
        send_sem=sends.at[slot],
        recv_sem=receives.at[slot],
        device_id={axis: peer},
        device_id_type=MESH,
    )
    copy.start()
    return copy


def params(number):
    return pltpu.CompilerParams(
        collective_id=number, has_side_effects=True, vmem_limit_bytes=40 * 1024 * 1024
    )


def sems(count):
    return [pltpu.SemaphoreType.DMA((count,)), pltpu.SemaphoreType.DMA((count,))]


VMEM = pl.BlockSpec(memory_space=pltpu.VMEM)
ANY = pl.BlockSpec(memory_space=pl.ANY)


def start_kernel(
    attn, small, ids, first, second,
    attn_all, small_all, ids_all, first_all, second_all,
    near_send, near_recv, far_send, far_recv, pass_send, pass_recv, here,
):
    section = lax.axis_index("section")
    expert = lax.axis_index("expert")
    other = 1 - section
    greet(["expert"], sibling=True)
    far = []
    for distance in range(1, PEERS):
        peer = around("expert", distance)
        far.append([
            send(attn, attn_all.at[section, expert], far_send, far_recv, 2 * distance - 2, "expert", peer),
            send(small, small_all.at[section, expert], far_send, far_recv, 2 * distance - 1, "expert", peer),
        ])
    pairs = [
        (attn, attn_all.at[section, expert]),
        (small, small_all.at[section, expert]),
        (ids, ids_all.at[section]),
        (first, first_all.at[section]),
        (second, second_all.at[section]),
    ]
    near = []
    own = []
    for slot, (source, target) in enumerate(pairs):
        near.append(send(source, target, near_send, near_recv, slot, "section", other))
        copy = pltpu.make_async_copy(source, target, here.at[slot])
        copy.start()
        own.append(copy)
    passed = []
    for distance in range(1, PEERS):
        origin = around("expert", PEERS - distance)
        for copy in far[distance - 1]:
            copy.wait_recv()
        for which, whole in enumerate((attn_all, small_all)):
            place = whole.at[section, origin]
            passed.append(
                send(place, place, pass_send, pass_recv, 2 * distance - 2 + which, "section", other)
            )
    for copy in own:
        copy.wait()
    for copy in near + passed:
        copy.wait()
    for group in far:
        for copy in group:
            copy.wait_send()


def collect_weights(attn, small, ids, first, second):
    if not use_kernels():
        over = lambda a: lax.all_gather(a, "section")
        return (
            over(lax.all_gather(attn, "expert")),
            over(lax.all_gather(small, "expert")),
            over(ids),
            over(first),
            over(second),
        )
    shapes = [
        (2, PEERS) + attn.shape,
        (2, PEERS) + small.shape,
        (2,) + ids.shape,
        (2,) + first.shape,
        (2,) + second.shape,
    ]
    return pl.pallas_call(
        start_kernel,
        out_shape=[jax.ShapeDtypeStruct(shape, jnp.bfloat16) for shape in shapes],
        in_specs=[ANY] * 5,
        out_specs=[ANY] * 5,
        scratch_shapes=sems(5) + sems(6) + sems(6) + [pltpu.SemaphoreType.DMA((5,))],
        compiler_params=params(1),
    )(attn, small, ids, first, second)


def total_kernel(part, whole, landed, send_one, recv_one, send_two, recv_two):
    own = lax.axis_index("tensor")
    greet(["tensor"])
    one = []
    for distance in range(1, PEERS):
        peer = around("tensor", distance)
        one.append(
            send(part.at[peer], landed.at[distance - 1], send_one, recv_one, distance - 1, "tensor", peer)
        )
    total = part[own].astype(jnp.float32)
    for slot, copy in enumerate(one):
        copy.wait_recv()
        total = total + landed[slot].astype(jnp.float32)
    whole[own] = total.astype(whole.dtype)
    two = []
    for distance in range(1, PEERS):
        peer = around("tensor", distance)
        two.append(
            send(whole.at[own], whole.at[own], send_two, recv_two, distance - 1, "tensor", peer)
        )
    for copy in two:
        copy.wait()
    for copy in one:
        copy.wait_send()


def sum_heads(part):
    if not use_kernels():
        return lax.psum(part, "tensor")
    length, width = part.shape
    split = part.reshape(PEERS, length // PEERS, width)
    return pl.pallas_call(
        total_kernel,
        out_shape=jax.ShapeDtypeStruct(split.shape, split.dtype),
        in_specs=[VMEM],
        out_specs=VMEM,
        scratch_shapes=[pltpu.VMEM((PEERS - 1,) + split.shape[1:], split.dtype)] + sems(3) + sems(3),
        compiler_params=params(2),
    )(split).reshape(length, width)


def joined(parts):
    count, groups, capacity, width = parts.shape
    return jnp.concatenate(
        [parts[index].reshape(groups * capacity, width) for index in range(count)], axis=-1
    )


def share_rows(own_rows, pick, rows, whole, first, second):
    own = lax.axis_index("tensor")
    expert = lax.axis_index("expert")
    rows[...] = (
        lax.dot_general(
            pick[...], own_rows[...], (((0,), (0,)), ((), ())), preferred_element_type=jnp.float32
        )
        .astype(rows.dtype)
        .reshape(rows.shape)
    )
    greet(["tensor", "expert"])
    one = []
    for distance in range(1, PEERS):
        peer = around("expert", distance)
        one.append(send(rows.at[peer], whole.at[own, expert], *first, distance - 1, "expert", peer))
    whole[own, expert] = rows[expert]
    for copy in one:
        copy.wait_recv()
    two = []
    for distance in range(1, PEERS):
        peer = around("tensor", distance)
        two.append(send(whole.at[own], whole.at[own], *second, distance - 1, "tensor", peer))
    for copy in two:
        copy.wait_recv()
    return one + two


def return_rows(values, pick, part, landed, reduced, arrived, back, out, first, second, third, beside):
    own = lax.axis_index("tensor")
    expert = lax.axis_index("expert")
    width = part.shape[3]
    for index in range(PEERS):
        part[index] = (
            values[:, index * width : (index + 1) * width].astype(part.dtype).reshape(part.shape[1:])
        )
    one = []
    for distance in range(1, PEERS):
        peer = around("tensor", distance)
        one.append(send(part.at[peer], landed.at[distance - 1], *first, distance - 1, "tensor", peer))
    if beside is not None:
        beside()
    for copy in one:
        copy.wait_recv()
    total = part[own].astype(jnp.float32)
    for slot in range(PEERS - 1):
        total = total + landed[slot].astype(jnp.float32)
    reduced[...] = total.astype(reduced.dtype)
    two = []
    for distance in range(1, PEERS):
        peer = around("expert", distance)
        two.append(send(reduced.at[peer], arrived.at[expert], *second, distance - 1, "expert", peer))
    arrived[expert] = reduced[expert]
    for copy in two:
        copy.wait_recv()
    groups, capacity, width = arrived.shape
    back[own] = jnp.dot(
        pick[...],
        arrived[...].reshape(groups * capacity, width),
        preferred_element_type=jnp.float32,
    ).astype(back.dtype)
    three = []
    for distance in range(1, PEERS):
        peer = around("tensor", distance)
        three.append(send(back.at[own], back.at[own], *third, distance - 1, "tensor", peer))
    for copy in three:
        copy.wait_recv()
    out[...] = jnp.concatenate([back[index] for index in range(PEERS)], axis=-1)
    return one + two + three


def expert_kernel(
    own_rows, pick, weight_in, weight_out,
    out, groups, hidden_out, active_out,
    rows, landed, part, reduced, arrived, back, whole, *pairs,
):
    pairs = [pairs[2 * index : 2 * index + 2] for index in range(5)]
    copies = share_rows(own_rows, pick, rows, whole, pairs[0], pairs[1])
    together = joined(whole)
    groups[...] = together
    hidden = jnp.dot(together, weight_in[...], preferred_element_type=jnp.float32)
    active = jax.nn.gelu(hidden).astype(jnp.bfloat16)
    values = jnp.dot(active, weight_out[...], preferred_element_type=jnp.float32)

    def keep():
        hidden_out[...] = hidden
        active_out[...] = active

    copies += return_rows(
        values, pick, part, landed, reduced, arrived, back, out, pairs[2], pairs[3], pairs[4], keep
    )
    for copy in copies:
        copy.wait_send()


def gelu_slope(values):
    scale = (2.0 / math.pi) ** 0.5
    square = values * values
    bent = jnp.tanh(scale * values * (1.0 + 0.044715 * square))
    return 0.5 * (1.0 + bent) + 0.5 * values * (1.0 - bent * bent) * scale * (
        1.0 + 3 * 0.044715 * square
    )


def expert_back_kernel(
    own_rows, pick, weight_in, weight_out, groups, hidden, active,
    out, grad_in, grad_out,
    rows, landed, part, reduced, arrived, back, whole, *pairs,
):
    pairs = [pairs[2 * index : 2 * index + 2] for index in range(5)]
    copies = share_rows(own_rows, pick, rows, whole, pairs[0], pairs[1])
    together = joined(whole)
    grad_active = lax.dot_general(
        together, weight_out[...], (((1,), (1,)), ((), ())), preferred_element_type=jnp.float32
    )
    grad_hidden = (grad_active * gelu_slope(hidden[...])).astype(jnp.bfloat16)
    values = lax.dot_general(
        grad_hidden, weight_in[...], (((1,), (1,)), ((), ())), preferred_element_type=jnp.float32
    )

    def weights():
        grad_in[...] = lax.dot_general(
            groups[...], grad_hidden, (((0,), (0,)), ((), ())), preferred_element_type=jnp.float32
        ).astype(grad_in.dtype)
        grad_out[...] = lax.dot_general(
            active[...], together, (((0,), (0,)), ((), ())), preferred_element_type=jnp.float32
        ).astype(grad_out.dtype)

    copies += return_rows(
        values, pick, part, landed, reduced, arrived, back, out, pairs[2], pairs[3], pairs[4], weights
    )
    for copy in copies:
        copy.wait_send()


def expert_call(kernel, number, outs, experts, capacity, operands):
    length, width = operands[0].shape
    low = jnp.bfloat16
    block = (experts, capacity, width)
    return pl.pallas_call(
        kernel,
        out_shape=outs,
        in_specs=[VMEM] * len(operands),
        out_specs=[VMEM] * len(outs),
        scratch_shapes=[
            pltpu.VMEM(block, low),
            pltpu.VMEM((PEERS - 1,) + block, low),
            pltpu.VMEM((PEERS,) + block, low),
            pltpu.VMEM(block, low),
            pltpu.VMEM(block, low),
            pltpu.VMEM((PEERS, length, width), low),
            pltpu.VMEM((PEERS,) + block, low),
        ]
        + sems(3) * 5,
        compiler_params=params(number),
    )(*operands)


def to_experts(own_rows, pick, experts, capacity):
    rows = lax.dot_general(
        pick, own_rows, (((0,), (0,)), ((), ())), preferred_element_type=jnp.float32
    ).astype(jnp.bfloat16)
    arrived = lax.all_to_all(
        rows.reshape(experts, capacity, -1), "expert", split_axis=0, concat_axis=0, tiled=True
    )
    return lax.all_gather(arrived.reshape(experts * capacity, -1), "tensor", axis=1, tiled=True)


def from_experts(values, pick, experts, capacity):
    share = lax.psum_scatter(
        values.astype(jnp.bfloat16), "tensor", scatter_dimension=1, tiled=True
    )
    returned = lax.all_to_all(
        share.reshape(experts, capacity, -1), "expert", split_axis=0, concat_axis=0, tiled=True
    )
    picked = jnp.dot(
        pick, returned.reshape(experts * capacity, -1), preferred_element_type=jnp.float32
    ).astype(jnp.bfloat16)
    return lax.all_gather(picked, "tensor", axis=1, tiled=True)


def run_experts(own_rows, pick, weight_in, weight_out, experts, capacity):
    if use_kernels():
        length = own_rows.shape[0]
        width, hidden_width = weight_in.shape
        slots = experts * capacity
        return expert_call(
            expert_kernel,
            3,
            [
                jax.ShapeDtypeStruct((length, width), jnp.bfloat16),
                jax.ShapeDtypeStruct((slots, width), jnp.bfloat16),
                jax.ShapeDtypeStruct((slots, hidden_width), jnp.float32),
                jax.ShapeDtypeStruct((slots, hidden_width), jnp.bfloat16),
            ],
            experts,
            capacity,
            (own_rows, pick, weight_in, weight_out),
        )
    groups = to_experts(own_rows, pick, experts, capacity)
    hidden = jnp.dot(groups, weight_in, preferred_element_type=jnp.float32)
    active = jax.nn.gelu(hidden).astype(jnp.bfloat16)
    values = jnp.dot(active, weight_out, preferred_element_type=jnp.float32)
    return (from_experts(values, pick, experts, capacity), groups, hidden, active)


def run_experts_back(
    own_rows, pick, weight_in, weight_out, groups, hidden, active, experts, capacity
):
    if use_kernels():
        return expert_call(
            expert_back_kernel,
            4,
            [
                jax.ShapeDtypeStruct((own_rows.shape[0], weight_in.shape[0]), jnp.bfloat16),
                jax.ShapeDtypeStruct(weight_in.shape, jnp.bfloat16),
                jax.ShapeDtypeStruct(weight_out.shape, jnp.bfloat16),
            ],
            experts,
            capacity,
            (own_rows, pick, weight_in, weight_out, groups, hidden, active),
        )
    grad_groups = to_experts(own_rows, pick, experts, capacity)
    grad_active = lax.dot_general(
        grad_groups, weight_out, (((1,), (1,)), ((), ())), preferred_element_type=jnp.float32
    )
    grad_hidden = (grad_active * gelu_slope(hidden)).astype(jnp.bfloat16)
    values = lax.dot_general(
        grad_hidden, weight_in, (((1,), (1,)), ((), ())), preferred_element_type=jnp.float32
    )
    grad_in = lax.dot_general(
        groups, grad_hidden, (((0,), (0,)), ((), ())), preferred_element_type=jnp.float32
    ).astype(jnp.bfloat16)
    grad_out = lax.dot_general(
        active, grad_groups, (((0,), (0,)), ((), ())), preferred_element_type=jnp.float32
    ).astype(jnp.bfloat16)
    return (from_experts(values, pick, experts, capacity), grad_in, grad_out)


def finish_kernel(
    normed, joint, attn, mixed, small, grads_out, small_out,
    give, give_small, came, came_small, summed, summed_small, landed, landed_small,
    near_send, near_recv, far_send, far_recv,
):
    section = lax.axis_index("section")
    expert = lax.axis_index("expert")
    other = 1 - section
    piece = summed.shape[1:3]
    columns = mixed.shape[2]

    def product(layer, index):
        pair = (normed[layer], joint[layer, index]) if index < 3 else (attn[layer], mixed[layer])
        whole = lax.dot_general(
            *pair, (((0,), (0,)), ((), ())), preferred_element_type=jnp.float32
        )
        return whole.reshape((PEERS, whole.shape[0] // PEERS, columns))

    for index in range(4):
        give[index] = product(other, index).astype(give.dtype)
    give_small[...] = small[other].astype(give_small.dtype)
    greet(["expert"], sibling=True)
    near = []
    for index in range(4):
        near.append(send(give.at[index], came.at[index], near_send, near_recv, index, "section", other))
    near.append(send(give_small, came_small, near_send, near_recv, 4, "section", other))
    copies = []
    near[4].wait_recv()
    summed_small[...] = (small[section] + came_small[...].astype(jnp.float32)).astype(summed_small.dtype)
    for distance in range(1, PEERS):
        peer = around("expert", distance)
        slot = distance - 1
        copies.append(
            (4, slot, send(summed_small.at[peer], landed_small.at[slot], far_send, far_recv, 12 + slot, "expert", peer))
        )
    for index in range(4):
        mine = product(section, index)
        near[index].wait_recv()
        summed[index] = (mine + came[index].astype(jnp.float32)).astype(summed.dtype)
        for distance in range(1, PEERS):
            peer = around("expert", distance)
            slot = distance - 1
            copies.append(
                (index, slot, send(summed.at[index, peer], landed.at[index, slot], far_send, far_recv, 3 * index + slot, "expert", peer))
            )
    small_out[...] = summed_small[expert].astype(jnp.float32)
    for index in range(4):
        grads_out[index] = summed[index, expert].astype(jnp.float32)
    for index, slot, copy in copies:
        copy.wait_recv()
        if index == 4:
            small_out[...] += landed_small[slot].astype(jnp.float32)
        else:
            grads_out[index] += landed[index, slot].astype(jnp.float32)
    for copy in near:
        copy.wait_send()
    for index, slot, copy in copies:
        copy.wait_send()


def reduce_grads(normed, joint, attn, mixed, small):
    experts = lax.axis_size("expert")
    layers, length, width = normed.shape
    piece = width // experts
    columns = mixed.shape[2]
    low = jnp.bfloat16
    if not use_kernels():
        section = lax.axis_index("section")
        outer = lambda a, b: jnp.einsum(
            "lta,ltb->lab", a, b, preferred_element_type=jnp.float32
        ).reshape(layers, experts, piece, columns)
        grads = jnp.stack(
            [outer(normed, joint[:, index]) for index in range(3)] + [outer(attn, mixed)], axis=2
        )
        results = []
        for part in (grads, small):
            scattered = lax.psum_scatter(
                part.astype(low), "expert", scatter_dimension=1, tiled=False
            ).astype(jnp.float32)
            own = lax.dynamic_index_in_dim(scattered, section, 0, keepdims=False)
            far = lax.dynamic_index_in_dim(scattered, 1 - section, 0, keepdims=False).astype(low)
            came = lax.ppermute(far, "section", [(0, 1), (1, 0)])
            results.append(own + came.astype(jnp.float32))
        return results
    return pl.pallas_call(
        finish_kernel,
        out_shape=[
            jax.ShapeDtypeStruct((4, piece, columns), jnp.float32),
            jax.ShapeDtypeStruct((piece, 128), jnp.float32),
        ],
        in_specs=[VMEM] * 5,
        out_specs=[VMEM] * 2,
        scratch_shapes=[
            pltpu.VMEM((4, PEERS, piece, columns), low),
            pltpu.VMEM((PEERS, piece, 128), low),
            pltpu.VMEM((4, PEERS, piece, columns), low),
            pltpu.VMEM((PEERS, piece, 128), low),
            pltpu.VMEM((4, PEERS, piece, columns), low),
            pltpu.VMEM((PEERS, piece, 128), low),
            pltpu.VMEM((4, PEERS - 1, piece, columns), low),
            pltpu.VMEM((PEERS - 1, piece, 128), low),
        ]
        + sems(5)
        + sems(15),
        compiler_params=params(5),
    )(normed, joint, attn, mixed, small)


def own_features(rows):
    width = rows.shape[1] // lax.axis_size("tensor")
    return lax.dynamic_slice_in_dim(rows, lax.axis_index("tensor") * width, width, 1)


def slots_for(length, experts):
    capacity = 5 * length // (4 * experts)
    return -(-capacity // 16) * 16


def offset_buckets(length):
    half_count = BUCKETS // 2
    exact_count = half_count // 2
    offsets = jnp.arange(2 * length, dtype=jnp.int32) - (length - 1)
    distance = jnp.abs(offsets)
    larger = jnp.full_like(distance, exact_count)
    for level_index in range(1, half_count - exact_count):
        border = int(
            math.ceil(
                exact_count * (128.0 / exact_count) ** (level_index / (half_count - exact_count))
                - 1e-09
            )
        )
        larger = larger + (distance >= border).astype(jnp.int32)
    bucket = jnp.where(distance < exact_count, distance, larger)
    return bucket + jnp.where(offsets > 0, half_count, 0)


def spread_offsets(per_offset, length):
    heads_here = per_offset.shape[0]
    tiled = jnp.tile(per_offset, (1, length))[:, : length * (2 * length - 1)]
    skewed = tiled.reshape(heads_here, length, 2 * length - 1)
    return skewed[:, :, length - 1 :]


def collect_offsets(grid_values, length):
    heads_here = grid_values.shape[0]
    padded = jnp.pad(grid_values, ((0, 0), (0, 0), (length - 1, 0)))
    flat = jnp.pad(padded.reshape(heads_here, length * (2 * length - 1)), ((0, 0), (0, length)))
    return jnp.sum(flat.reshape(heads_here, length, 2 * length), axis=1, dtype=jnp.float32)


def rms_scale(values, gain_vector):
    return (
        values * lax.rsqrt(jnp.mean(values * values, axis=-1, keepdims=True) + 1e-06) * gain_vector
    )


def slot_places(route_ids, experts, capacity):
    chosen = route_ids[:, None] == jnp.arange(experts, dtype=jnp.int32)[None, :]
    counts = jnp.cumsum(chosen.astype(jnp.int32), axis=0)
    slot_number = jnp.sum(jnp.where(chosen, counts, 0), axis=-1) - 1
    return (chosen, route_ids * capacity + slot_number)


def position_bias(offset_table, bias_table, length):
    per_offset = jnp.dot(
        offset_table, bias_table.astype(jnp.float32), precision=lax.Precision.HIGHEST
    )
    return spread_offsets(per_offset.T, length)


def attention_probs(query_heads, key_heads, rel_bias, labels, head_size):
    scores = (
        jnp.einsum("qhe,khe->hqk", query_heads, key_heads, preferred_element_type=jnp.float32)
        * head_size ** (-0.5)
        + rel_bias
    )
    same_doc = labels[:, None] == labels[None, :]
    return jnp.where(same_doc[None], scores, -1000000000.0)


def forward_layer(layer_in, weights, route_ids, labels, offset_table, weight_in, weight_out):
    gain_one, joint_weight, attn_out_weight, bias_table, gain_two, router_matrix = weights
    length, model_width = layer_in.shape
    heads_here = bias_table.shape[1]
    head_size = attn_out_weight.shape[1] // heads_here
    experts = router_matrix.shape[1]
    capacity = slots_for(length, experts)
    input_float = layer_in.astype(jnp.float32)
    normed = rms_scale(input_float, gain_one).astype(jnp.bfloat16)
    joint_heads = jnp.dot(normed, joint_weight, preferred_element_type=jnp.float32).astype(
        jnp.bfloat16
    )
    query_heads, key_heads, value_heads = [
        part.reshape(length, heads_here, head_size) for part in jnp.split(joint_heads, 3, axis=1)
    ]
    rel_bias = position_bias(offset_table, bias_table, length)
    scores = attention_probs(query_heads, key_heads, rel_bias, labels, head_size)
    log_total = jax.nn.logsumexp(scores, axis=-1)
    probs_low = jnp.exp(scores - log_total[..., None]).astype(jnp.bfloat16)
    mixed_heads = (
        jnp.einsum("hqk,khe->qhe", probs_low, value_heads, preferred_element_type=jnp.float32)
        .astype(jnp.bfloat16)
        .reshape(length, heads_here * head_size)
    )
    partial_out = lax.dot_general(
        mixed_heads, attn_out_weight, (((1,), (1,)), ((), ())), preferred_element_type=jnp.float32
    )
    residual = input_float + sum_heads(partial_out.astype(jnp.bfloat16)).astype(jnp.float32)
    normed_two = rms_scale(residual, gain_two)
    logits = jnp.dot(normed_two, router_matrix, precision=lax.Precision.HIGHEST)
    router_probs = jax.nn.softmax(logits, axis=-1)
    chosen, slot_index = slot_places(route_ids, experts, capacity)
    gate_value = jnp.sum(jnp.where(chosen, router_probs, 0.0), axis=-1, keepdims=True)
    pick = (
        slot_index[:, None] == jnp.arange(experts * capacity, dtype=jnp.int32)[None, :]
    ).astype(jnp.bfloat16)
    expert_low, groups, hidden, active = run_experts(
        own_features(normed_two).astype(jnp.bfloat16),
        pick,
        weight_in,
        weight_out,
        experts,
        capacity,
    )
    output = (residual + gate_value * expert_low.astype(jnp.float32)).astype(jnp.bfloat16)
    kept_state = (
        layer_in,
        normed,
        query_heads,
        key_heads,
        value_heads,
        mixed_heads,
        log_total,
        residual,
        router_probs,
        gate_value,
        pick,
        groups,
        hidden,
        active,
        expert_low,
    )
    return (output, kept_state)


def backward_layer(
    grad_out, kept_state, weights, route_ids, labels, offset_table, weight_in, weight_out
):
    (
        layer_in,
        normed,
        query_heads,
        key_heads,
        value_heads,
        mixed_heads,
        log_total,
        residual,
        router_probs,
        gate_value,
        pick,
        groups,
        hidden,
        active,
        expert_low,
    ) = kept_state
    gain_one, joint_weight, attn_out_weight, bias_table, gain_two, router_matrix = weights
    length, model_width = layer_in.shape
    heads_here = bias_table.shape[1]
    head_size = attn_out_weight.shape[1] // heads_here
    experts = router_matrix.shape[1]
    capacity = slots_for(length, experts)
    grad_float = grad_out.astype(jnp.float32)
    grad_gate = jnp.sum(grad_float * expert_low.astype(jnp.float32), axis=-1, keepdims=True)
    grad_value = (gate_value * grad_float).astype(jnp.bfloat16)
    grad_rows, grad_weight_in, grad_weight_out = run_experts_back(
        own_features(grad_value),
        pick,
        weight_in,
        weight_out,
        groups,
        hidden,
        active,
        experts,
        capacity,
    )
    grad_normed_two = grad_rows.astype(jnp.float32)
    chosen = route_ids[:, None] == jnp.arange(experts, dtype=jnp.int32)[None, :]
    grad_logits = grad_gate * gate_value * (chosen.astype(jnp.float32) - router_probs)
    grad_normed_two = grad_normed_two + lax.dot_general(
        grad_logits, router_matrix, (((1,), (1,)), ((), ())), precision=lax.Precision.HIGHEST
    )
    normed_two, norm_pull = jax.vjp(rms_scale, residual, gain_two)
    grad_router = lax.dot_general(
        normed_two, grad_logits, (((0,), (0,)), ((), ())), precision=lax.Precision.HIGHEST
    )
    grad_residual, grad_gain_two = norm_pull(grad_normed_two)
    grad_residual = grad_residual + grad_float
    grad_attn = grad_residual.astype(jnp.bfloat16)
    grad_mixed = (
        jnp.dot(grad_attn, attn_out_weight, preferred_element_type=jnp.float32)
        .astype(jnp.bfloat16)
        .reshape(length, heads_here, head_size)
    )
    rel_bias = position_bias(offset_table, bias_table, length)
    scores = attention_probs(query_heads, key_heads, rel_bias, labels, head_size)
    probs_float = jnp.exp(scores - log_total[..., None])
    probs_low = probs_float.astype(jnp.bfloat16)
    grad_probs = jnp.einsum(
        "qhe,khe->hqk", grad_mixed, value_heads, preferred_element_type=jnp.float32
    )
    grad_scores = (
        probs_float * (grad_probs - jnp.sum(probs_float * grad_probs, axis=-1, keepdims=True))
    ).astype(jnp.bfloat16)
    grad_query = (
        jnp.einsum("hqk,khe->qhe", grad_scores, key_heads, preferred_element_type=jnp.float32)
        * head_size ** (-0.5)
    ).astype(jnp.bfloat16)
    grad_keys = (
        jnp.einsum("hqk,qhe->khe", grad_scores, query_heads, preferred_element_type=jnp.float32)
        * head_size ** (-0.5)
    ).astype(jnp.bfloat16)
    grad_values = jnp.einsum(
        "hqk,qhe->khe", probs_low, grad_mixed, preferred_element_type=jnp.float32
    ).astype(jnp.bfloat16)
    offset_sums = collect_offsets(grad_scores, length)
    grad_table = jnp.einsum("kb,hk->bh", offset_table, offset_sums, precision=lax.Precision.HIGHEST)
    grad_joint = jnp.concatenate(
        [
            part.reshape(length, heads_here * head_size)
            for part in (grad_query, grad_keys, grad_values)
        ],
        axis=1,
    )
    grad_normed_part = lax.dot_general(
        grad_joint, joint_weight, (((1,), (1,)), ((), ())), preferred_element_type=jnp.float32
    )
    grad_normed = sum_heads(grad_normed_part.astype(jnp.bfloat16)).astype(jnp.float32)
    input_pull = jax.vjp(rms_scale, layer_in.astype(jnp.float32), gain_one)[1]
    grad_input_part, grad_gain_one = input_pull(grad_normed)
    grad_input = (grad_residual + grad_input_part).astype(jnp.bfloat16)
    small_terms = (grad_gain_one, grad_table, grad_gain_two, grad_router)
    joint_terms = jnp.stack(
        [
            part.reshape(length, heads_here * head_size)
            for part in (grad_query, grad_keys, grad_values)
        ]
    )
    return (
        grad_input,
        small_terms,
        (normed, joint_terms, grad_attn, mixed_heads),
        (grad_weight_in, grad_weight_out),
    )


def pack_terms(small_terms, expert_count):
    gain_one, table, gain_two, router = small_terms
    width = gain_one.shape[0]
    piece = width // expert_count
    rows = table.shape[0] // expert_count
    table = jnp.pad(
        table.reshape(expert_count, rows, -1), ((0, 0), (0, piece - rows), (0, 0))
    ).reshape(width, -1)
    used = 2 + table.shape[1] + router.shape[1]
    return jnp.concatenate(
        [
            gain_one[:, None],
            gain_two[:, None],
            table,
            router,
            jnp.zeros((width, 128 - used), jnp.float32),
        ],
        axis=1,
    ).reshape(expert_count, piece, 128)


def swap_micro(per_layer):
    section = lax.axis_index("section")
    own = jnp.where(section == 0, per_layer[0], per_layer[1])
    other = jnp.where(section == 0, per_layer[1], per_layer[0])
    came = lax.ppermute(other, "section", [(0, 1), (1, 0)])
    return jnp.where(
        section == 0, jnp.stack([own, came]), jnp.stack([came, own])
    )[None]


def local(
    inputs,
    cotangent,
    attn_gain,
    query_weight,
    key_weight,
    value_weight,
    out_weight,
    rel_table,
    ffn_gain,
    router_weight,
    expert_in,
    expert_out,
    routes,
    segments,
):
    section = lax.axis_index("section")
    layers = lax.axis_size("section")
    expert_count = lax.axis_size("expert")
    micro_count, length, model_width = inputs.shape
    heads_here = rel_table.shape[2]
    experts = router_weight.shape[2]
    piece = attn_gain.shape[1]
    attn = jnp.concatenate([query_weight, key_weight, value_weight, out_weight], axis=0)
    used = 2 + heads_here + experts
    small = jnp.concatenate(
        [
            attn_gain[0][:, None],
            ffn_gain[0][:, None],
            jnp.pad(rel_table[0], ((0, piece - rel_table.shape[1]), (0, 0))),
            router_weight[0],
            jnp.zeros((piece, 128 - used), jnp.bfloat16),
        ],
        axis=1,
    )
    ids = jnp.pad(routes[0, :, :, 0].astype(jnp.bfloat16), ((0, 16 - micro_count), (0, 0)))
    attn_all, small_all, ids_all, in_all, out_all = collect_weights(
        attn, small, ids, expert_in[0, 0], expert_out[0, 0]
    )
    offset_ids = offset_buckets(length)
    offset_table = (offset_ids[:, None] == jnp.arange(BUCKETS, dtype=jnp.int32)[None, :]).astype(
        jnp.float32
    )
    labels = lax.dynamic_index_in_dim(segments, section, 0, keepdims=False)
    current = lax.dynamic_index_in_dim(inputs, section, 0, keepdims=False)
    layer_weights = []
    kept_list = []
    outputs = []
    for layer in range(layers):
        matrices = attn_all[layer]
        columns = small_all[layer]
        flat = columns.reshape(model_width, -1)
        weights = (
            flat[:, 0].astype(jnp.float32),
            jnp.concatenate(
                [matrices[:, which].reshape(model_width, -1) for which in range(3)], axis=1
            ),
            matrices[:, 3].reshape(model_width, -1),
            columns[:, : rel_table.shape[1], 2 : 2 + heads_here].reshape(BUCKETS, heads_here),
            flat[:, 1].astype(jnp.float32),
            flat[:, 2 + heads_here : used].astype(jnp.float32),
        )
        route_ids = lax.dynamic_index_in_dim(ids_all[layer], section, 0, keepdims=False).astype(
            jnp.int32
        )
        layer_weights.append((weights, route_ids))
        current, kept_state = forward_layer(
            current, weights, route_ids, labels, offset_table, in_all[layer], out_all[layer]
        )
        kept_list.append(kept_state)
        outputs.append(current)
    grad = lax.dynamic_index_in_dim(cotangent, section, 0, keepdims=False)
    input_grads = [None] * layers
    packs = [None] * layers
    expert_packs = [None] * layers
    for layer in reversed(range(layers)):
        weights, route_ids = layer_weights[layer]
        grad, small_terms, wide_terms, expert_terms = backward_layer(
            grad,
            kept_list[layer],
            weights,
            route_ids,
            labels,
            offset_table,
            in_all[layer],
            out_all[layer],
        )
        input_grads[layer] = grad
        packs[layer] = wide_terms + (pack_terms(small_terms, expert_count),)
        expert_packs[layer] = expert_terms
    came = [
        jax.tree.map(
            lambda a: lax.ppermute(a, "section", [(1 - layer, layer)]), expert_packs[layer]
        )
        for layer in range(layers)
    ]
    grads, small_grads = reduce_grads(*[jnp.stack(pair) for pair in zip(*packs)])
    grad_in, grad_out = [
        jnp.where(section == 0, expert_packs[0][index], expert_packs[1][index]).astype(jnp.float32)
        + jnp.where(section == 0, came[0][index], came[1][index]).astype(jnp.float32)
        for index in range(2)
    ]
    return (
        swap_micro(outputs),
        swap_micro(input_grads),
        small_grads[None, :, 0],
        grads[0][None],
        grads[1][None],
        grads[2][None],
        grads[3][None],
        small_grads[None, : rel_table.shape[1], 2 : 2 + heads_here],
        small_grads[None, :, 1],
        small_grads[None, :, 2 + heads_here : used],
        grad_in[None, None],
        grad_out[None, None],
    )


def solution(mesh):
    return jax.shard_map(
        local,
        mesh=mesh,
        in_specs=(
            P(None, "expert", None),
            P(None, "expert", None),
            P("section", "expert"),
            P("section", "expert", "tensor"),
            P("section", "expert", "tensor"),
            P("section", "expert", "tensor"),
            P("section", "expert", "tensor"),
            P("section", "expert", "tensor"),
            P("section", "expert"),
            P("section", "expert", None),
            P("section", "expert", None, "tensor"),
            P("section", "expert", "tensor", None),
            P("section", None, "expert", None),
            P(None, "expert"),
        ),
        out_specs=(
            P("section", None, "expert", None),
            P("section", None, "expert", None),
            P("section", "expert"),
            P("section", "expert", "tensor"),
            P("section", "expert", "tensor"),
            P("section", "expert", "tensor"),
            P("section", "expert", "tensor"),
            P("section", "expert", "tensor"),
            P("section", "expert"),
            P("section", "expert", None),
            P("section", "expert", None, "tensor"),
            P("section", "expert", "tensor", None),
        ),
        check_vma=False,
    )
```

profile of v0, /device:TPU:0, one launch (start us, length us, event | category | flops | bytes accessed | tf_op | source)
XLA Modules:
  0.0 359.7 jit_solution(15834934789041493274)
XLA Ops:
  0.7 1.1 fusion.25
  6.3 1.1 pad_maximum_fusion.3.attn
  7.6 1.3 copy-done.12
  8.9 37.4 %shard_map.229 = (bf16[2,4,4,192,192]{4,3,2,1,0:T(8,128)(2,1)S(1)}, bf16[2,4,192,128]{3,2,1,0:T(8,128)(2,1)S(1)}, bf16[2,16,128]{2,1,0:T(8,128)(2,1)S(1)}, bf16[...) custom-call(bf16[4,192,192]{2,1,0:T(8,128)(2,1)S(1)} %pad_maximum_fusion.3.attn, ...), custom_call_target="tpu_custom_call" | custom-call | tf_op jit(solution)/shard_map/pallas_call | solution.py:142
  46.3 2.2 slice_bitcast_fusion
  50.7 3.1 fusion.130
  57.4 10.6 %shard_map.230 = bf16[4,32,768]{2,1,0:T(8,128)(2,1)S(1)} custom-call(bf16[4,32,768]{2,1,0:T(8,128)(2,1)S(1)} %bitcast.284), custom_call_target="tpu_custom_call" | custom-call | tf_op jit(solution)/shard_map/pallas_call | solution.py:183
  69.8 1.1 select_reduce_fusion.3
  73.0 3.7 %slice_bitcast_fusion.2 = (bf16[768,768]{1,0:T(8,128)(2,1)S(1)}, bf16[768,768]{1,0:T(8,128)(2,1)S(1)}, bf16[768,768]{1,0:T(8,128)(2,1)S(1)}, bf16[768,768]{1,0:T(8,128)(2,1)}) fusion(bf16[2,768,768]{2,1,0:T(8,128)(2,1)} %copy-done.10, bf16[2,768,768]{2,1,0:T(8,128)(2,1)} %copy-done.9), kind=kLoop, calls=%fused_computation.7 | loop fusion | bytes 9437184 | tf_op jit(solution)/shard_map/squeeze | solution.py:891
  76.8 35.2 %shard_map.231 = (bf16[128,768]{1,0:T(8,128)(2,1)S(1)}, bf16[192,768]{1,0:T(8,128)(2,1)S(1)}, f32[192,768]{1,0:T(8,128)S(1)}, bf16[192,768]{1,0:T(8,128)(2,1)S(1)}) custom-call(bf16[128,192]{1,0:T(8,128)(2,1)S(1)} %copy-done.25, bf16[128,192]{1,0:T(8,128)(2,1)S(1)} %fusion.64.pick, bf16[768,768]{1,0:T(8,128)(2,1)S(1)} %get-tuple-element.153.weight_in, ...), custom_call_target="tpu_custom_call" | custom-call | tf_op jit(solution)/shard_map/pallas_call | solution.py:338
  115.8 1.6 copy.125
  118.1 2.2 convolution_convert_fusion.4
  123.1 2.3 reshape.564
  125.5 1.8 slice.176
  127.3 1.7 copy.126
  129.0 1.3 fusion.140
  131.3 1.3 convolution_convert_fusion
  132.6 9.5 %shard_map.232 = bf16[4,32,768]{2,1,0:T(8,128)(2,1)S(1)} custom-call(bf16[4,32,768]{2,1,0:T(8,128)(2,1)S(1)} %bitcast.285), custom_call_target="tpu_custom_call" | custom-call | tf_op jit(solution)/shard_map/pallas_call | solution.py:183
  143.6 1.0 copy.127
  144.6 1.2 multiply_multiply_fusion
  145.9 1.6 fusion.141
  147.6 1.0 bitcast_convert_fusion
  149.5 25.2 %shard_map.233 = (bf16[128,768]{1,0:T(8,128)(2,1)S(1)}, bf16[192,768]{1,0:T(8,128)(2,1)S(1)}, f32[192,768]{1,0:T(8,128)S(1)}, bf16[192,768]{1,0:T(8,128)(2,1)S(1)}) custom-call(bf16[128,192]{1,0:T(8,128)(2,1)S(1)} %dynamic-slice_convert_fusion.own_rows, bf16[128,192]{1,0:T(8,128)(2,1)S(1)} %fusion.65.pick, bf16[768,768]{1,0:T(8,128)(2,1)S(1)} %copy-done.2, ...), custom_call_target="tpu_custom_call" | custom-call | tf_op jit(solution)/shard_map/pallas_call | solution.py:338
  175.4 28.2 %shard_map.234 = (bf16[128,768]{1,0:T(8,128)(2,1)S(1)}, bf16[768,768]{1,0:T(8,128)(2,1)}, bf16[768,768]{1,0:T(8,128)(2,1)}) custom-call(bf16[128,192]{1,0:T(8,128)(2,1)S(1)} %fusion.61.own_rows, bf16[128,192]{1,0:T(8,128)(2,1)S(1)} %fusion.65.pick, bf16[768,768]{1,0:T(8,128)(2,1)S(1)} %copy-done.2, bf16[768,768]{1,0:T(8,128)(2,1)S(1)} %get-tuple-element.104.weight_out, ...), custom_call_target="tpu_custom_call" | custom-call | tf_op jit(solution)/shard_map/pallas_call | solution.py:338
  203.8 1.2 multiply_reduce_fusion
  207.8 10.4 %shard_map.235 = bf16[4,32,768]{2,1,0:T(8,128)(2,1)S(1)} custom-call(bf16[4,32,768]{2,1,0:T(8,128)(2,1)S(1)} %bitcast.286), custom_call_target="tpu_custom_call" | custom-call | tf_op jit(solution)/shard_map/pallas_call | solution.py:183
  218.4 1.4 fusion.21
  220.1 27.0 %shard_map.236 = (bf16[128,768]{1,0:T(8,128)(2,1)S(1)}, bf16[768,768]{1,0:T(8,128)(2,1)}, bf16[768,768]{1,0:T(8,128)(2,1)}) custom-call(bf16[128,192]{1,0:T(8,128)(2,1)S(1)} %fusion.60.own_rows, bf16[128,192]{1,0:T(8,128)(2,1)S(1)} %copy-done.18, bf16[768,768]{1,0:T(8,128)(2,1)S(1)} %get-tuple-element.153.weight_in, ...), custom_call_target="tpu_custom_call" | custom-call | tf_op jit(solution)/shard_map/pallas_call | solution.py:338
  247.1 1.4 collective-permute-start.4
  248.6 5.1 %collective-permute-start.5 = (bf16[768,768]{1,0:T(8,128)(2,1)}, bf16[768,768]{1,0:T(8,128)(2,1)}, u32[]{:S(2)}, u32[]{:S(2)}) collective-permute-start(bf16[768,768]{1,0:T(8,128)(2,1)} %get-tuple-element.53), channel_id=1, source_target_pairs={{0,16},{1,17},{2,18},{3,19},{4,20},{5,21},{6,22},{7,23},{8,24},{9,... | collective-permute-start | bytes 3538952 | tf_op jit(solution)/shard_map/ppermute | solution.py:916
  253.7 1.3 collective-permute-start.2
  255.0 5.1 %collective-permute-start.3 = (bf16[768,768]{1,0:T(8,128)(2,1)}, bf16[768,768]{1,0:T(8,128)(2,1)}, u32[]{:S(2)}, u32[]{:S(2)}) collective-permute-start(bf16[768,768]{1,0:T(8,128)(2,1)} %get-tuple-element.51), channel_id=1, source_target_pairs={{0,16},{1,17},{2,18},{3,19},{4,20},{5,21},{6,22},{7,23},{8,24},{9,... | collective-permute-start | bytes 3538952 | tf_op jit(solution)/shard_map/ppermute | solution.py:916
  260.8 2.0 multiply_reduce_fusion.1
  263.5 1.5 convert_bitcast_fusion.1
  267.5 10.4 %shard_map.237 = bf16[4,32,768]{2,1,0:T(8,128)(2,1)S(1)} custom-call(bf16[4,32,768]{2,1,0:T(8,128)(2,1)S(1)} %bitcast.287), custom_call_target="tpu_custom_call" | custom-call | tf_op jit(solution)/shard_map/pallas_call | solution.py:183
  285.6 1.5 copy.91
  287.1 1.5 copy.90
  288.7 1.5 copy.84
  290.2 1.5 copy.85
  291.7 1.5 copy.86
  293.2 1.5 copy.87
  294.8 1.5 copy.88
  296.3 1.5 copy.89
  297.8 1.6 concatenate.80
  301.7 44.8 %shard_map.238 = (f32[4,192,192]{2,1,0:T(8,128)S(1)}, f32[192,128]{1,0:T(8,128)S(1)}) custom-call(bf16[2,128,768]{2,1,0:T(8,128)(2,1)S(1)} %pad_maximum_fusion.4.normed, bf16[2,3,128,192]{3,2,1,0:T(8,128)(2,1)S(1)} %pad_maximum_fusion.5.joint, bf16[2,128,768]{2,1,0:T(8,128)(2,1)S(1)} %pad_maximum_fusion.6.attn, ...), custom_call_target="tpu_custom_call" | custom-call | tf_op jit(solution)/shard_map/pallas_call | solution.py:522
  349.9 1.8 maximum_select_fusion.1
  352.6 3.6 add_bitcast_fusion
  356.2 3.6 add_bitcast_fusion.1
  (409 shorter events, 45.6 us)
Async XLA Ops:
  0.6 54.2 %copy-start = (s32[2,128]{1,0:T(2,128)S(1)}, s32[2,128]{1,0:T(2,128)}, u32[]{:S(2)}) copy-start(s32[2,128]{1,0:T(2,128)} %param.27) | copy-start | bytes 3076
  0.7 54.3 %copy-start.126 = (s32[256]{0:T(256)}, s32[256]{0:T(256)S(1)}, u32[]{:S(2)}) copy-start(s32[256]{0:T(256)S(1)} %fusion.101) | copy-start | bytes 3076
  2.3 51.5 %copy-start.105 = (f32[128]{0:T(128)}, f32[128]{0:T(128)S(1)}, u32[]{:S(2)}) copy-start(f32[128]{0:T(128)S(1)} %fusion.115) | copy-start | bytes 1540
  50.3 18.8 %copy-start.43 = (bf16[1,4,192,128]{3,2,1,0:T(8,128)(2,1)}, bf16[1,4,192,128]{3,2,1,0:T(8,128)(2,1)S(1)}, u32[]{:S(2)}) copy-start(bf16[1,4,192,128]{3,2,1,0:T(8,128)(2,1)S(1)} %get-tuple-element.125) | copy-start | bytes 589828
  56.8 12.8 %copy-start.92 = (f32[3,128]{1,0:T(4,128)}, f32[3,128]{1,0:T(4,128)S(1)}, u32[]{:S(2)}) copy-start(f32[3,128]{1,0:T(4,128)S(1)} %log_add_fusion.1) | copy-start | bytes 4612
  57.0 14.6 %copy-start.56 = (bf16[3,64,128]{2,1,0:T(8,128)(2,1)}, bf16[3,64,128]{2,1,0:T(8,128)(2,1)S(1)}, u32[]{:S(2)}) copy-start(bf16[3,64,128]{2,1,0:T(8,128)(2,1)S(1)} %convolution_convert_fusion.9) | copy-start | bytes 147460
  76.8 36.7 %copy-start.7 = (bf16[4,32,768]{2,1,0:T(8,128)(2,1)S(1)}, bf16[4,32,768]{2,1,0:T(8,128)(2,1)}, u32[]{:S(2)}) copy-start(bf16[4,32,768]{2,1,0:T(8,128)(2,1)} %copy-done.6) | copy-start | bytes 589828
  76.8 36.7 %copy-start.34 = (bf16[2,128,768]{2,1,0:T(8,128)(2,1)S(1)}, bf16[2,128,768]{2,1,0:T(8,128)(2,1)}, u32[]{:S(2)}) copy-start(bf16[2,128,768]{2,1,0:T(8,128)(2,1)} %param.14) | copy-start | bytes 1179652
  76.8 36.7 %copy-start.109 = (f32[128]{0:T(128)S(1)}, f32[128]{0:T(128)}, u32[]{:S(2)}) copy-start(f32[128]{0:T(128)} %get-tuple-element.100) | copy-start | bytes 1540
  76.8 38.2 %copy-start.45 = (bf16[1,4,192,128]{3,2,1,0:T(8,128)(2,1)S(1)}, bf16[1,4,192,128]{3,2,1,0:T(8,128)(2,1)}, u32[]{:S(2)}) copy-start(bf16[1,4,192,128]{3,2,1,0:T(8,128)(2,1)} %get-tuple-element.124) | copy-start | bytes 589828
  129.0 13.9 %copy-start.26 = (bf16[128,768]{1,0:T(8,128)(2,1)S(1)}, bf16[128,768]{1,0:T(8,128)(2,1)}, u32[]{:S(2)}) copy-start(bf16[128,768]{1,0:T(8,128)(2,1)} %get-tuple-element.99) | copy-start | bytes 589828
  130.3 12.8 %copy-start.31 = (f32[3,128,128]{1,2,0:T(8,128)}, f32[3,128,128]{1,2,0:T(8,128)S(1)}, u32[]{:S(2)}) copy-start(f32[3,128,128]{1,2,0:T(8,128)S(1)} %get-tuple-element.144) | copy-start | bytes 589828
  131.3 16.3 %copy-start.102 = (s32[128]{0:T(128)S(1)}, s32[128]{0:T(128)}, u32[]{:S(2)}) copy-start(s32[128]{0:T(128)} %copy-done.101) | copy-start | bytes 1540
  147.6 27.4 %copy-start.107 = (f32[128]{0:T(128)}, f32[128]{0:T(128)S(1)}, u32[]{:S(2)}) copy-start(f32[128]{0:T(128)S(1)} %get-tuple-element.96) | copy-start | bytes 1540
  147.6 27.1 %copy-start.50 = (bf16[2,128,768]{2,1,0:T(8,128)(2,1)S(1)}, bf16[2,128,768]{2,1,0:T(8,128)(2,1)}, u32[]{:S(2)}) copy-start(bf16[2,128,768]{2,1,0:T(8,128)(2,1)} %param.15) | copy-start | bytes 1179652
  175.0 28.6 %copy-start.120 = (f32[128]{0:T(128)}, f32[128]{0:T(128)S(1)}, u32[]{:S(2)}) copy-start(f32[128]{0:T(128)S(1)} %mul.403) | copy-start | bytes 1540
  175.4 28.3 %copy-start.4 = (bf16[4,32,768]{2,1,0:T(8,128)(2,1)S(1)}, bf16[4,32,768]{2,1,0:T(8,128)(2,1)}, u32[]{:S(2)}) copy-start(bf16[4,32,768]{2,1,0:T(8,128)(2,1)} %copy-done.3) | copy-start | bytes 589828
  175.4 28.3 %copy-start.27 = (bf16[128,768]{1,0:T(8,128)(2,1)S(1)}, bf16[128,768]{1,0:T(8,128)(2,1)}, u32[]{:S(2)}) copy-start(bf16[128,768]{1,0:T(8,128)(2,1)} %get-tuple-element.99) | copy-start | bytes 589828
  175.4 28.3 %copy-start.46 = (bf16[1,4,192,128]{3,2,1,0:T(8,128)(2,1)S(1)}, bf16[1,4,192,128]{3,2,1,0:T(8,128)(2,1)}, u32[]{:S(2)}) copy-start(bf16[1,4,192,128]{3,2,1,0:T(8,128)(2,1)} %get-tuple-element.124) | copy-start | bytes 589828
  175.4 28.3 %copy-start.115 = (f32[128]{0:T(128)S(1)}, f32[128]{0:T(128)}, u32[]{:S(2)}) copy-start(f32[128]{0:T(128)} %copy-done.114) | copy-start | bytes 1540
  175.4 29.5 %copy-start.123 = (f32[128]{0:T(128)S(1)}, f32[128]{0:T(128)}, u32[]{:S(2)}) copy-start(f32[128]{0:T(128)} %copy-done.122) | copy-start | bytes 1540
  207.1 11.3 %copy-start.125 = (f32[128]{0:T(128)S(1)}, f32[128]{0:T(128)}, u32[]{:S(2)}) copy-start(f32[128]{0:T(128)} %copy-done.124) | copy-start | bytes 1540
  207.1 11.3 %copy-start.16 = (bf16[128,768]{1,0:T(8,128)(2,1)S(1)}, bf16[128,768]{1,0:T(8,128)(2,1)}, u32[]{:S(2)}) copy-start(bf16[128,768]{1,0:T(8,128)(2,1)} %copy-done.15) | copy-start | bytes 589828
  207.7 12.1 %copy-start.110 = (f32[128]{0:T(128)S(1)}, f32[128]{0:T(128)}, u32[]{:S(2)}) copy-start(f32[128]{0:T(128)} %get-tuple-element.100) | copy-start | bytes 1540
  207.7 12.3 %copy-start.18 = (bf16[128,192]{1,0:T(8,128)(2,1)S(1)}, bf16[128,192]{1,0:T(8,128)(2,1)}, u32[]{:S(2)}) copy-start(bf16[128,192]{1,0:T(8,128)(2,1)} %copy-done.17) | copy-start | bytes 147460
  207.8 12.3 %copy-start.20 = (f32[192,768]{1,0:T(8,128)S(1)}, f32[192,768]{1,0:T(8,128)}, u32[]{:S(2)}) copy-start(f32[192,768]{1,0:T(8,128)} %copy-done.19) | copy-start | bytes 1769476
  207.8 12.3 %copy-start.22 = (bf16[192,768]{1,0:T(8,128)(2,1)S(1)}, bf16[192,768]{1,0:T(8,128)(2,1)}, u32[]{:S(2)}) copy-start(bf16[192,768]{1,0:T(8,128)(2,1)} %copy-done.21) | copy-start | bytes 884740
  207.8 12.3 %copy-start.24 = (bf16[192,768]{1,0:T(8,128)(2,1)S(1)}, bf16[192,768]{1,0:T(8,128)(2,1)}, u32[]{:S(2)}) copy-start(bf16[192,768]{1,0:T(8,128)(2,1)} %copy-done.23) | copy-start | bytes 884740
  220.0 40.7 %copy-start.8 = (bf16[4,32,768]{2,1,0:T(8,128)(2,1)S(1)}, bf16[4,32,768]{2,1,0:T(8,128)(2,1)}, u32[]{:S(2)}) copy-start(bf16[4,32,768]{2,1,0:T(8,128)(2,1)} %copy-done.6) | copy-start | bytes 589828
  220.1 40.7 %copy-start.35 = (bf16[2,128,768]{2,1,0:T(8,128)(2,1)S(1)}, bf16[2,128,768]{2,1,0:T(8,128)(2,1)}, u32[]{:S(2)}) copy-start(bf16[2,128,768]{2,1,0:T(8,128)(2,1)} %param.14) | copy-start | bytes 1179652
  220.1 40.7 %copy-start.44 = (bf16[1,4,192,128]{3,2,1,0:T(8,128)(2,1)S(1)}, bf16[1,4,192,128]{3,2,1,0:T(8,128)(2,1)}, u32[]{:S(2)}) copy-start(bf16[1,4,192,128]{3,2,1,0:T(8,128)(2,1)} %copy-done.43) | copy-start | bytes 589828
  220.1 40.7 %copy-start.95 = (f32[768]{0:T(1024)S(1)}, f32[768]{0:T(1024)}, u32[]{:S(2)}) copy-start(f32[768]{0:T(1024)} %copy-done.94) | copy-start | bytes 9220
  220.1 40.7 %copy-start.98 = (f32[128,4]{0,1:T(4,128)S(1)}, f32[128,4]{0,1:T(4,128)}, u32[]{:S(2)}) copy-start(f32[128,4]{0,1:T(4,128)} %get-tuple-element.101) | copy-start | bytes 6148
  247.1 17.9 %copy-start.41 = (bf16[4,1,192,192]{3,2,1,0:T(8,128)(2,1)S(1)}, bf16[4,1,192,192]{3,2,1,0:T(8,128)(2,1)}, u32[]{:S(2)}) copy-start(bf16[4,1,192,192]{3,2,1,0:T(8,128)(2,1)} %copy-done.40) | copy-start | bytes 884740
  247.1 105.4 %collective-permute-start.4 = (bf16[768,768]{1,0:T(8,128)(2,1)}, bf16[768,768]{1,0:T(8,128)(2,1)}, u32[]{:S(2)}, u32[]{:S(2)}) collective-permute-start(bf16[768,768]{1,0:T(8,128)(2,1)} %get-tuple-element.52), channel_id=1, source_target_pairs={{16,0},{17,1},{18,2},{19,3},{20,4},{21,5},{22,6},{23,7},{24,8},{25... | collective-permute-start | bytes 3538952 | tf_op jit(solution)/shard_map/ppermute | solution.py:916
  248.6 104.0 %collective-permute-start.5 = (bf16[768,768]{1,0:T(8,128)(2,1)}, bf16[768,768]{1,0:T(8,128)(2,1)}, u32[]{:S(2)}, u32[]{:S(2)}) collective-permute-start(bf16[768,768]{1,0:T(8,128)(2,1)} %get-tuple-element.53), channel_id=1, source_target_pairs={{0,16},{1,17},{2,18},{3,19},{4,20},{5,21},{6,22},{7,23},{8,24},{9,... | collective-permute-start | bytes 3538952 | tf_op jit(solution)/shard_map/ppermute | solution.py:916
  253.7 102.5 %collective-permute-start.2 = (bf16[768,768]{1,0:T(8,128)(2,1)}, bf16[768,768]{1,0:T(8,128)(2,1)}, u32[]{:S(2)}, u32[]{:S(2)}) collective-permute-start(bf16[768,768]{1,0:T(8,128)(2,1)} %get-tuple-element.50), channel_id=1, source_target_pairs={{16,0},{17,1},{18,2},{19,3},{20,4},{21,5},{22,6},{23,7},{24,8},{25... | collective-permute-start | bytes 3538952 | tf_op jit(solution)/shard_map/ppermute | solution.py:916
  255.0 101.2 %collective-permute-start.3 = (bf16[768,768]{1,0:T(8,128)(2,1)}, bf16[768,768]{1,0:T(8,128)(2,1)}, u32[]{:S(2)}, u32[]{:S(2)}) collective-permute-start(bf16[768,768]{1,0:T(8,128)(2,1)} %get-tuple-element.51), channel_id=1, source_target_pairs={{0,16},{1,17},{2,18},{3,19},{4,20},{5,21},{6,22},{7,23},{8,24},{9,... | collective-permute-start | bytes 3538952 | tf_op jit(solution)/shard_map/ppermute | solution.py:916
  266.9 11.2 %copy-start.118 = (f32[128]{0:T(128)S(1)}, f32[128]{0:T(128)}, u32[]{:S(2)}) copy-start(f32[128]{0:T(128)} %copy-done.117) | copy-start | bytes 1540
  267.4 12.4 %copy-start.39 = (f32[128,768]{1,0:T(8,128)S(1)}, f32[128,768]{1,0:T(8,128)}, u32[]{:S(2)}) copy-start(f32[128,768]{1,0:T(8,128)} %copy-done.38) | copy-start | bytes 1179652
  267.5 12.4 %copy-start.103 = (s32[128]{0:T(128)S(1)}, s32[128]{0:T(128)}, u32[]{:S(2)}) copy-start(s32[128]{0:T(128)} %copy-done.101) | copy-start | bytes 1540
  267.5 12.4 %copy-start.121 = (f32[128]{0:T(128)S(1)}, f32[128]{0:T(128)}, u32[]{:S(2)}) copy-start(f32[128]{0:T(128)} %copy-done.120) | copy-start | bytes 1540
  279.7 69.4 %collective-permute-start.1 = (bf16[128,768]{1,0:T(8,128)(2,1)}, bf16[128,768]{1,0:T(8,128)(2,1)}, u32[]{:S(2)}, u32[]{:S(2)}) collective-permute-start(bf16[128,768]{1,0:T(8,128)(2,1)} %broadcast_select_fusion), channel_id=1, source_target_pairs={{0,16},{16,0},{1,17},{17,1},{2,18},{18,2},{3,19},{19,3},{4,20},{20... | collective-permute-start | bytes 589832 | tf_op jit(solution)/shard_map/ppermute | solution.py:818
  301.7 47.2 %copy-start.5 = (bf16[4,32,768]{2,1,0:T(8,128)(2,1)S(1)}, bf16[4,32,768]{2,1,0:T(8,128)(2,1)}, u32[]{:S(2)}) copy-start(bf16[4,32,768]{2,1,0:T(8,128)(2,1)} %copy-done.3) | copy-start | bytes 589828
  301.7 47.2 %copy-start.14 = (bf16[128,768]{1,0:T(8,128)(2,1)S(1)}, bf16[128,768]{1,0:T(8,128)(2,1)}, u32[]{:S(2)}) copy-start(bf16[128,768]{1,0:T(8,128)(2,1)} %copy-done.13) | copy-start | bytes 589828
  301.7 47.2 %copy-start.28 = (bf16[128,768]{1,0:T(8,128)(2,1)S(1)}, bf16[128,768]{1,0:T(8,128)(2,1)}, u32[]{:S(2)}) copy-start(bf16[128,768]{1,0:T(8,128)(2,1)} %get-tuple-element.99) | copy-start | bytes 589828
  301.7 47.2 %copy-start.108 = (f32[128]{0:T(128)S(1)}, f32[128]{0:T(128)}, u32[]{:S(2)}) copy-start(f32[128]{0:T(128)} %copy-done.107) | copy-start | bytes 1540
  349.1 2.7 collective-permute-start
  (87 other events, 206.9 us)
where the time goes:
time: 361 us; the launch traced here: 360 us
  Pallas kernels  239 us (66%)
  local copies, waits for them, and re-layouts  56.3 us (16%)
  other arithmetic  30.1 us (8%)
  matrix products  18.6 us (5%)
  starting transfers between devices  13 us (4%)
    pallas_call x4, Pallas kernels, expert_call(): pl.pallas_call(kernel, out_shape=outs, in_specs=[VMEM] * len(operands), o...  116 us
    pallas_call x1, Pallas kernels, reduce_grads(): pl.pallas_call(finish_kernel, out_shape=[jax.ShapeDtypeStruct((4, piece,...  44.8 us
    pallas_call x4, Pallas kernels, sum_heads(): pl.pallas_call(total_kernel, out_shape=jax.ShapeDtypeStruct(split.shape,...  40.9 us
    pallas_call x1, Pallas kernels, collect_weights(): pl.pallas_call(start_kernel, out_shape=[jax.ShapeDtypeStruct(shape, jnp.b...  37.4 us
    unnamed x273, local copies, waits for them, and re-layouts  16.3 us
    ppermute x4, starting transfers between devices, local(): lax.ppermute(a, 'section', [(1 - layer, layer)])  13 us
    another operation x6, local copies, waits for them, and re-layouts, backward_layer(): jnp.stack([part.reshape(length, heads_here * head_size) for part in (grad...  9.14 us
  transfers between devices with their start and end apart: 6, of which 0 were waited for; matrix products, arithmetic and copies ran while one was open for 11% of the time, Pallas kernels for 15%

commit v1 on v0

--- a/solution.py
+++ b/solution.py
@@ -436,78 +436,88 @@
 
 
 def finish_kernel(
-    normed, joint, attn, mixed, small, grads_out, small_out,
+    normed, joint, attn, mixed, small, give_in, give_out,
+    grads_out, small_out, came_in, came_out,
     give, give_small, came, came_small, summed, summed_small, landed, landed_small,
     near_send, near_recv, far_send, far_recv,
 ):
     section = lax.axis_index("section")
     expert = lax.axis_index("expert")
     other = 1 - section
-    piece = summed.shape[1:3]
-    columns = mixed.shape[2]
-
-    def product(layer, index):
-        pair = (normed[layer], joint[layer, index]) if index < 3 else (attn[layer], mixed[layer])
-        whole = lax.dot_general(
-            *pair, (((0,), (0,)), ((), ())), preferred_element_type=jnp.float32
-        )
-        return whole.reshape((PEERS, whole.shape[0] // PEERS, columns))
-
-    for index in range(4):
-        give[index] = product(other, index).astype(give.dtype)
+
+    def product(layer):
+        dims = (((0,), (0,)), ((), ()))
+        left = lax.dot_general(
+            normed[layer], joint[layer], dims, preferred_element_type=jnp.float32
+        )
+        right = lax.dot_general(
+            attn[layer], mixed[layer], dims, preferred_element_type=jnp.float32
+        )
+        return jnp.concatenate([left, right], axis=-1).reshape(summed.shape)
+
+    give[...] = product(other).astype(give.dtype)
     give_small[...] = small[other].astype(give_small.dtype)
     greet(["expert"], sibling=True)
     near = []
-    for index in range(4):
-        near.append(send(give.at[index], came.at[index], near_send, near_recv, index, "section", other))
+    for distance in range(PEERS):
+        peer = around("expert", distance)
+        near.append(
+            send(give.at[peer], came.at[peer], near_send, near_recv, distance, "section", other)
+        )
     near.append(send(give_small, came_small, near_send, near_recv, 4, "section", other))
+    near.append(send(give_in, came_in, near_send, near_recv, 5, "section", other))
+    near.append(send(give_out, came_out, near_send, near_recv, 6, "section", other))
+    summed[...] = product(section).astype(summed.dtype)
     copies = []
+    for distance in (1, 2, 3, 0):
+        peer = around("expert", distance)
+        near[distance].wait_recv()
+        summed[peer] = (
+            summed[peer].astype(jnp.float32) + came[peer].astype(jnp.float32)
+        ).astype(summed.dtype)
+        if distance:
+            slot = distance - 1
+            copies.append(
+                send(summed.at[peer], landed.at[slot], far_send, far_recv, slot, "expert", peer)
+            )
     near[4].wait_recv()
-    summed_small[...] = (small[section] + came_small[...].astype(jnp.float32)).astype(summed_small.dtype)
+    summed_small[...] = (small[section] + came_small[...].astype(jnp.float32)).astype(
+        summed_small.dtype
+    )
     for distance in range(1, PEERS):
         peer = around("expert", distance)
         slot = distance - 1
         copies.append(
-            (4, slot, send(summed_small.at[peer], landed_small.at[slot], far_send, far_recv, 12 + slot, "expert", peer))
-        )
-    for index in range(4):
-        mine = product(section, index)
-        near[index].wait_recv()
-        summed[index] = (mine + came[index].astype(jnp.float32)).astype(summed.dtype)
-        for distance in range(1, PEERS):
-            peer = around("expert", distance)
-            slot = distance - 1
-            copies.append(
-                (index, slot, send(summed.at[index, peer], landed.at[index, slot], far_send, far_recv, 3 * index + slot, "expert", peer))
+            send(
+                summed_small.at[peer], landed_small.at[slot], far_send, far_recv, 3 + slot, "expert", peer
             )
+        )
+    grads_out[...] = summed[expert].astype(jnp.float32)
     small_out[...] = summed_small[expert].astype(jnp.float32)
-    for index in range(4):
-        grads_out[index] = summed[index, expert].astype(jnp.float32)
-    for index, slot, copy in copies:
-        copy.wait_recv()
-        if index == 4:
-            small_out[...] += landed_small[slot].astype(jnp.float32)
-        else:
-            grads_out[index] += landed[index, slot].astype(jnp.float32)
-    for copy in near:
+    for slot in range(PEERS - 1):
+        copies[slot].wait_recv()
+        grads_out[...] += landed[slot].astype(jnp.float32)
+        copies[3 + slot].wait_recv()
+        small_out[...] += landed_small[slot].astype(jnp.float32)
+    near[5].wait_recv()
+    near[6].wait_recv()
+    for copy in near + copies:
         copy.wait_send()
-    for index, slot, copy in copies:
-        copy.wait_send()
-
-
-def reduce_grads(normed, joint, attn, mixed, small):
+
+
+def reduce_grads(normed, joint, attn, mixed, small, give_in, give_out):
     experts = lax.axis_size("expert")
     layers, length, width = normed.shape
     piece = width // experts
-    columns = mixed.shape[2]
+    columns = joint.shape[2] + mixed.shape[2]
     low = jnp.bfloat16
     if not use_kernels():
         section = lax.axis_index("section")
         outer = lambda a, b: jnp.einsum(
             "lta,ltb->lab", a, b, preferred_element_type=jnp.float32
-        ).reshape(layers, experts, piece, columns)
-        grads = jnp.stack(
-            [outer(normed, joint[:, index]) for index in range(3)] + [outer(attn, mixed)], axis=2
+        )
+        grads = jnp.concatenate([outer(normed, joint), outer(attn, mixed)], axis=2).reshape(
+            layers, experts, piece, columns
         )
         results = []
         for part in (grads, small):
@@ -518,29 +528,29 @@
             far = lax.dynamic_index_in_dim(scattered, 1 - section, 0, keepdims=False).astype(low)
             came = lax.ppermute(far, "section", [(0, 1), (1, 0)])
             results.append(own + came.astype(jnp.float32))
-        return results
+        swap = lambda a: lax.ppermute(a, "section", [(0, 1), (1, 0)])
+        return results + [swap(give_in), swap(give_out)]
+    wide = (PEERS, piece, columns)
+    slim = (PEERS, piece, 128)
     return pl.pallas_call(
         finish_kernel,
         out_shape=[
-            jax.ShapeDtypeStruct((4, piece, columns), jnp.float32),
+            jax.ShapeDtypeStruct((piece, columns), jnp.float32),
             jax.ShapeDtypeStruct((piece, 128), jnp.float32),
+            jax.ShapeDtypeStruct(give_in.shape, low),
+            jax.ShapeDtypeStruct(give_out.shape, low),
         ],
-        in_specs=[VMEM] * 5,
-        out_specs=[VMEM] * 2,
-        scratch_shapes=[
-            pltpu.VMEM((4, PEERS, piece, columns), low),
-            pltpu.VMEM((PEERS, piece, 128), low),
-            pltpu.VMEM((4, PEERS, piece, columns), low),
-            pltpu.VMEM((PEERS, piece, 128), low),
-            pltpu.VMEM((4, PEERS, piece, columns), low),
-            pltpu.VMEM((PEERS, piece, 128), low),
-            pltpu.VMEM((4, PEERS - 1, piece, columns), low),
+        in_specs=[VMEM] * 7,
+        out_specs=[VMEM] * 4,
+        scratch_shapes=[pltpu.VMEM(shape, low) for _ in range(3) for shape in (wide, slim)]
+        + [
+            pltpu.VMEM((PEERS - 1, piece, columns), low),
             pltpu.VMEM((PEERS - 1, piece, 128), low),
         ]
-        + sems(5)
-        + sems(15),
+        + sems(7)
+        + sems(6),
         compiler_params=params(5),
-    )(normed, joint, attn, mixed, small)
+    )(normed, joint, attn, mixed, small, give_in, give_out)
 
 
 def own_features(rows):
@@ -776,16 +786,10 @@
     grad_input_part, grad_gain_one = input_pull(grad_normed)
     grad_input = (grad_residual + grad_input_part).astype(jnp.bfloat16)
     small_terms = (grad_gain_one, grad_table, grad_gain_two, grad_router)
-    joint_terms = jnp.stack(
-        [
-            part.reshape(length, heads_here * head_size)
-            for part in (grad_query, grad_keys, grad_values)
-        ]
-    )
     return (
         grad_input,
         small_terms,
-        (normed, joint_terms, grad_attn, mixed_heads),
+        (normed, grad_joint, grad_attn, mixed_heads),
         (grad_weight_in, grad_weight_out),
     )
 
@@ -844,7 +848,10 @@
     heads_here = rel_table.shape[2]
     experts = router_weight.shape[2]
     piece = attn_gain.shape[1]
-    attn = jnp.concatenate([query_weight, key_weight, value_weight, out_weight], axis=0)
+    attn = jnp.concatenate(
+        [query_weight[0], key_weight[0], value_weight[0], out_weight[0]], axis=1
+    )
+    joint_columns = 3 * query_weight.shape[2]
     used = 2 + heads_here + experts
     small = jnp.concatenate(
         [
@@ -870,15 +877,13 @@
     kept_list = []
     outputs = []
     for layer in range(layers):
-        matrices = attn_all[layer]
+        matrices = attn_all[layer].reshape(model_width, -1)
         columns = small_all[layer]
         flat = columns.reshape(model_width, -1)
         weights = (
             flat[:, 0].astype(jnp.float32),
-            jnp.concatenate(
-                [matrices[:, which].reshape(model_width, -1) for which in range(3)], axis=1
-            ),
-            matrices[:, 3].reshape(model_width, -1),
+            matrices[:, :joint_columns],
+            matrices[:, joint_columns:],
             columns[:, : rel_table.shape[1], 2 : 2 + heads_here].reshape(BUCKETS, heads_here),
             flat[:, 1].astype(jnp.float32),
             flat[:, 2 + heads_here : used].astype(jnp.float32),
@@ -911,26 +916,27 @@
         input_grads[layer] = grad
         packs[layer] = wide_terms + (pack_terms(small_terms, expert_count),)
         expert_packs[layer] = expert_terms
-    came = [
-        jax.tree.map(
-            lambda a: lax.ppermute(a, "section", [(1 - layer, layer)]), expert_packs[layer]
-        )
-        for layer in range(layers)
-    ]
-    grads, small_grads = reduce_grads(*[jnp.stack(pair) for pair in zip(*packs)])
-    grad_in, grad_out = [
-        jnp.where(section == 0, expert_packs[0][index], expert_packs[1][index]).astype(jnp.float32)
-        + jnp.where(section == 0, came[0][index], came[1][index]).astype(jnp.float32)
+    given = [
+        jnp.where(section == 0, expert_packs[1][index], expert_packs[0][index])
         for index in range(2)
     ]
+    kept = [
+        jnp.where(section == 0, expert_packs[0][index], expert_packs[1][index])
+        for index in range(2)
+    ]
+    grads, small_grads, *came = reduce_grads(*[jnp.stack(pair) for pair in zip(*packs)], *given)
+    grad_in, grad_out = [
+        kept[index].astype(jnp.float32) + came[index].astype(jnp.float32) for index in range(2)
+    ]
+    parts = jnp.split(grads, 4, axis=1)
     return (
         swap_micro(outputs),
         swap_micro(input_grads),
         small_grads[None, :, 0],
-        grads[0][None],
-        grads[1][None],
-        grads[2][None],
-        grads[3][None],
+        parts[0][None],
+        parts[1][None],
+        parts[2][None],
+        parts[3][None],
         small_grads[None, : rel_table.shape[1], 2 : 2 + heads_here],
         small_grads[None, :, 1],
         small_grads[None, :, 2 + heads_here : used],

time: 361 us -> 338 us (0.936)
  Pallas kernels: 239 us -> 219 us
  starting transfers between devices: 13 us -> 0.54 us
  matrix products: 18.6 us -> 23.4 us
    ppermute x4 -> x0, starting transfers between devices: 13 us -> none  [local(): lax.ppermute(a, 'section', [(1 - layer, layer)])]
    another operation x6 -> x0, local copies, waits for them, and re-layouts: 9.14 us -> none  [backward_layer(): jnp.stack([part.reshape(length, heads_here * head_size) for part in (grad...]
    pallas_call x1, Pallas kernels: 44.8 us -> 36.4 us  [reduce_grads(): pl.pallas_call(finish_kernel, out_shape=[jax.ShapeDtypeStruct((piece, col...]
    concatenate x9, local copies, waits for them, and re-layouts: 3.56 us -> 11.5 us  [pack_terms(): jnp.concatenate([gain_one[:, None], gain_two[:, None], table, router, jnp...]
    pallas_call x1, Pallas kernels: 37.4 us -> 30.8 us  [collect_weights(): pl.pallas_call(start_kernel, out_shape=[jax.ShapeDtypeStruct(shape, jnp.b...]
    unnamed x273 -> x297, local copies, waits for them, and re-layouts: 16.3 us -> 19.7 us
  transfers between devices with their start and end apart: 6 -> 2, of which waited for: 0 -> 0; matrix products, arithmetic and copies ran while one was open for 11% -> 10% of each run, Pallas kernels for 15% -> 11%
where the time goes in v1:
time: 338 us; the launch traced here: 336 us
  Pallas kernels  219 us (65%)
  local copies, waits for them, and re-layouts  57.1 us (17%)
  other arithmetic  33.3 us (10%)
  matrix products  23.4 us (7%)
    pallas_call x4, Pallas kernels, expert_call(): pl.pallas_call(kernel, out_shape=outs, in_specs=[VMEM] * len(operands), o...  112 us
    pallas_call x4, Pallas kernels, sum_heads(): pl.pallas_call(total_kernel, out_shape=jax.ShapeDtypeStruct(split.shape,...  39.6 us
    pallas_call x1, Pallas kernels, reduce_grads(): pl.pallas_call(finish_kernel, out_shape=[jax.ShapeDtypeStruct((piece, col...  36.4 us
    pallas_call x1, Pallas kernels, collect_weights(): pl.pallas_call(start_kernel, out_shape=[jax.ShapeDtypeStruct(shape, jnp.b...  30.8 us
    unnamed x297, local copies, waits for them, and re-layouts  19.7 us
    concatenate x9, local copies, waits for them, and re-layouts, pack_terms(): jnp.concatenate([gain_one[:, None], gain_two[:, None], table, router, jnp...  11.5 us
  transfers between devices with their start and end apart: 2, of which 0 were waited for; matrix products, arithmetic and copies ran while one was open for 10% of the time, Pallas kernels for 11%

profile of v1, /device:TPU:0, one launch (start us, length us, event | category | flops | bytes accessed | tf_op | source)
XLA Modules:
  0.0 336.3 jit_solution(1152985057635862287)
XLA Ops:
  1.2 1.0 fusion.29
  6.8 1.9 pad_maximum_fusion.4.attn
  9.5 1.3 copy-done.19
  12.5 30.8 %shard_map.229 = (bf16[2,4,192,768]{3,2,1,0:T(8,128)(2,1)S(1)}, bf16[2,4,192,128]{3,2,1,0:T(8,128)(2,1)S(1)}, bf16[2,16,128]{2,1,0:T(8,128)(2,1)S(1)}, bf16[2,76...) custom-call(bf16[192,768]{1,0:T(8,128)(2,1)S(1)} %copy-done.20, bf16[192,128]{1,0:T(8,128)(2,1)S(1)} %copy-done.35, ...), custom_call_target="tpu_custom_call" | custom-call | tf_op jit(solution)/shard_map/pallas_call | solution.py:142
  43.3 1.4 copy-done.16
  44.7 1.4 copy-done.17
  48.0 1.2 fusion.128
  52.4 1.4 convolution_convert_fusion.3
  53.9 10.7 %shard_map.230 = bf16[4,32,768]{2,1,0:T(8,128)(2,1)S(1)} custom-call(bf16[4,32,768]{2,1,0:T(8,128)(2,1)S(1)} %bitcast.270), custom_call_target="tpu_custom_call" | custom-call | tf_op jit(solution)/shard_map/pallas_call | solution.py:183
  69.0 3.7 %slice_bitcast_fusion = (bf16[768,768]{1,0:T(8,128)(2,1)S(1)}, bf16[768,768]{1,0:T(8,128)(2,1)S(1)}, bf16[768,768]{1,0:T(8,128)(2,1)S(1)}, bf16[768,768]{1,0:T(8,128)(2,1)}) fusion(bf16[2,768,768]{2,1,0:T(8,128)(2,1)} %copy-done.17, bf16[2,768,768]{2,1,0:T(8,128)(2,1)} %copy-done.16), kind=kLoop, calls=%fused_computation.5 | loop fusion | bytes 9437184 | tf_op jit(solution)/shard_map/squeeze | solution.py:896
  72.7 33.1 %shard_map.231 = (bf16[128,768]{1,0:T(8,128)(2,1)S(1)}, bf16[192,768]{1,0:T(8,128)(2,1)S(1)}, f32[192,768]{1,0:T(8,128)S(1)}, bf16[192,768]{1,0:T(8,128)(2,1)S(1)}) custom-call(bf16[128,192]{1,0:T(8,128)(2,1)S(1)} %copy-done.34, bf16[128,192]{1,0:T(8,128)(2,1)S(1)} %fusion.62.pick, bf16[768,768]{1,0:T(8,128)(2,1)S(1)} %get-tuple-element.149.weight_in, ...), custom_call_target="tpu_custom_call" | custom-call | tf_op jit(solution)/shard_map/pallas_call | solution.py:338
  109.7 1.0 copy.125
  110.7 1.9 convolution_convert_fusion.4
  115.4 2.3 reshape.564
  117.7 1.8 slice.140
  119.5 1.7 copy.126
  121.3 1.3 fusion.136
  123.6 1.4 convolution_convert_fusion.2
  125.0 9.5 %shard_map.232 = bf16[4,32,768]{2,1,0:T(8,128)(2,1)S(1)} custom-call(bf16[4,32,768]{2,1,0:T(8,128)(2,1)S(1)} %bitcast.271), custom_call_target="tpu_custom_call" | custom-call | tf_op jit(solution)/shard_map/pallas_call | solution.py:183
  135.9 1.6 copy.127
  138.4 1.1 multiply_multiply_fusion
  139.5 1.6 fusion.137
  143.7 25.3 %shard_map.233 = (bf16[128,768]{1,0:T(8,128)(2,1)S(1)}, bf16[192,768]{1,0:T(8,128)(2,1)S(1)}, f32[192,768]{1,0:T(8,128)S(1)}, bf16[192,768]{1,0:T(8,128)(2,1)S(1)}) custom-call(bf16[128,192]{1,0:T(8,128)(2,1)S(1)} %dynamic-slice_convert_fusion.own_rows, bf16[128,192]{1,0:T(8,128)(2,1)S(1)} %fusion.63.pick, bf16[768,768]{1,0:T(8,128)(2,1)S(1)} %copy-done.1, ...), custom_call_target="tpu_custom_call" | custom-call | tf_op jit(solution)/shard_map/pallas_call | solution.py:338
  169.7 27.7 %shard_map.234 = (bf16[128,768]{1,0:T(8,128)(2,1)S(1)}, bf16[768,768]{1,0:T(8,128)(2,1)S(1)}, bf16[768,768]{1,0:T(8,128)(2,1)S(1)}) custom-call(bf16[128,192]{1,0:T(8,128)(2,1)S(1)} %fusion.59.own_rows, bf16[128,192]{1,0:T(8,128)(2,1)S(1)} %fusion.63.pick, bf16[768,768]{1,0:T(8,128)(2,1)S(1)} %copy-done.1, ...), custom_call_target="tpu_custom_call" | custom-call | tf_op jit(solution)/shard_map/pallas_call | solution.py:338
  197.5 1.3 multiply_reduce_fusion
  199.7 1.5 convolution_convert_fusion.11
  202.6 1.7 convolution_convert_fusion.1
  204.2 9.9 %shard_map.235 = bf16[4,32,768]{2,1,0:T(8,128)(2,1)S(1)} custom-call(bf16[4,32,768]{2,1,0:T(8,128)(2,1)S(1)} %bitcast.272), custom_call_target="tpu_custom_call" | custom-call | tf_op jit(solution)/shard_map/pallas_call | solution.py:183
  215.8 26.3 %shard_map.236 = (bf16[128,768]{1,0:T(8,128)(2,1)S(1)}, bf16[768,768]{1,0:T(8,128)(2,1)S(1)}, bf16[768,768]{1,0:T(8,128)(2,1)S(1)}) custom-call(bf16[128,192]{1,0:T(8,128)(2,1)S(1)} %fusion.58.own_rows, bf16[128,192]{1,0:T(8,128)(2,1)S(1)} %copy-done.27, bf16[768,768]{1,0:T(8,128)(2,1)S(1)} %get-tuple-element.149.weight_in, ...), custom_call_target="tpu_custom_call" | custom-call | tf_op jit(solution)/shard_map/pallas_call | solution.py:338
  242.2 1.2 multiply_reduce_fusion.1
  247.4 1.3 convolution_convert_fusion
  248.7 9.5 %shard_map.237 = bf16[4,32,768]{2,1,0:T(8,128)(2,1)S(1)} custom-call(bf16[4,32,768]{2,1,0:T(8,128)(2,1)S(1)} %bitcast.273), custom_call_target="tpu_custom_call" | custom-call | tf_op jit(solution)/shard_map/pallas_call | solution.py:183
  261.9 1.6 fusion.93
  266.1 1.2 convolution_bitcast_fusion
  269.2 1.0 concatenate.78
  270.3 1.0 concatenate.79
  274.2 1.0 concatenate.81
  276.7 1.2 broadcast_select_fusion.give_out
  278.4 1.1 broadcast_select_fusion.1.give_in
  280.3 2.5 concatenate.72
  282.8 2.5 concatenate.77
  285.4 1.3 pad_maximum_fusion.small
  288.4 36.4 %shard_map.238 = (f32[192,768]{1,0:T(8,128)S(1)}, f32[192,128]{1,0:T(8,128)S(1)}, bf16[768,768]{1,0:T(8,128)(2,1)S(1)}, bf16[768,768]{1,0:T(8,128)(2,1)S(1)}) custom-call(bf16[2,128,768]{2,1,0:T(8,128)(2,1)S(1)} %pad_maximum_fusion.1.normed, bf16[2,128,576]{2,1,0:T(8,128)(2,1)S(1)} %pad_maximum_fusion.3.joint, ...), custom_call_target="tpu_custom_call" | custom-call | tf_op jit(solution)/shard_map/pallas_call | solution.py:535
  324.9 1.8 add_bitcast_fusion
  326.7 1.8 add_bitcast_fusion.1
  330.9 1.8 slice_reduce_fusion
  332.7 1.8 maximum_select_fusion.1
  334.5 1.8 maximum_select_fusion
  (426 shorter events, 54.9 us)
Async XLA Ops:
  0.6 49.2 %copy-start = (s32[2,128]{1,0:T(2,128)S(1)}, s32[2,128]{1,0:T(2,128)}, u32[]{:S(2)}) copy-start(s32[2,128]{1,0:T(2,128)} %param.27) | copy-start | bytes 3076
  0.7 8.8 %copy-start.18 = (bf16[1,1,768,768]{3,2,1,0:T(8,128)(2,1)S(1)}, bf16[1,1,768,768]{3,2,1,0:T(8,128)(2,1)}, u32[]{:S(2)}) copy-start(bf16[1,1,768,768]{3,2,1,0:T(8,128)(2,1)} %param.24) | copy-start | bytes 3538948
  47.0 18.5 %copy-start.56 = (bf16[1,4,192,128]{3,2,1,0:T(8,128)(2,1)}, bf16[1,4,192,128]{3,2,1,0:T(8,128)(2,1)S(1)}, u32[]{:S(2)}) copy-start(bf16[1,4,192,128]{3,2,1,0:T(8,128)(2,1)S(1)} %get-tuple-element.121) | copy-start | bytes 589828
  51.5 13.8 %copy-start.66 = (bf16[768,1]{1,0:T(8,128)(2,1)S(1)}, bf16[768,1]{1,0:T(8,128)(2,1)}, u32[]{:S(2)}) copy-start(bf16[768,1]{1,0:T(8,128)(2,1)} %get-tuple-element.125) | copy-start | bytes 4612
  51.9 13.5 %copy-start.98 = (f32[3,128]{1,0:T(4,128)}, f32[3,128]{1,0:T(4,128)S(1)}, u32[]{:S(2)}) copy-start(f32[3,128]{1,0:T(4,128)S(1)} %log_add_fusion.1) | copy-start | bytes 4612
  52.4 13.0 %copy-start.72 = (bf16[3,64,128]{2,1,0:T(8,128)(2,1)}, bf16[3,64,128]{2,1,0:T(8,128)(2,1)S(1)}, u32[]{:S(2)}) copy-start(bf16[3,64,128]{2,1,0:T(8,128)(2,1)S(1)} %convolution_convert_fusion.9) | copy-start | bytes 147460
  66.8 40.5 %copy-start.117 = (f32[128]{0:T(128)}, f32[128]{0:T(128)S(1)}, u32[]{:S(2)}) copy-start(f32[128]{0:T(128)S(1)} %get-tuple-element.104) | copy-start | bytes 1540
  72.7 34.6 %copy-start.3 = (bf16[4,32,768]{2,1,0:T(8,128)(2,1)S(1)}, bf16[4,32,768]{2,1,0:T(8,128)(2,1)}, u32[]{:S(2)}) copy-start(bf16[4,32,768]{2,1,0:T(8,128)(2,1)} %copy-done.2) | copy-start | bytes 589828
  72.7 34.6 %copy-start.45 = (bf16[2,128,768]{2,1,0:T(8,128)(2,1)S(1)}, bf16[2,128,768]{2,1,0:T(8,128)(2,1)}, u32[]{:S(2)}) copy-start(bf16[2,128,768]{2,1,0:T(8,128)(2,1)} %param.14) | copy-start | bytes 1179652
  72.7 36.1 %copy-start.58 = (bf16[1,4,192,128]{3,2,1,0:T(8,128)(2,1)S(1)}, bf16[1,4,192,128]{3,2,1,0:T(8,128)(2,1)}, u32[]{:S(2)}) copy-start(bf16[1,4,192,128]{3,2,1,0:T(8,128)(2,1)} %get-tuple-element.120) | copy-start | bytes 589828
  121.3 14.0 %copy-start.36 = (bf16[128,768]{1,0:T(8,128)(2,1)S(1)}, bf16[128,768]{1,0:T(8,128)(2,1)}, u32[]{:S(2)}) copy-start(bf16[128,768]{1,0:T(8,128)(2,1)} %get-tuple-element.103) | copy-start | bytes 589828
  122.5 12.9 %copy-start.42 = (f32[3,128,128]{1,2,0:T(8,128)}, f32[3,128,128]{1,2,0:T(8,128)S(1)}, u32[]{:S(2)}) copy-start(f32[3,128,128]{1,2,0:T(8,128)S(1)} %get-tuple-element.140) | copy-start | bytes 589828
  123.6 12.3 %copy-start.74 = (bf16[3,64,128]{2,1,0:T(8,128)(2,1)}, bf16[3,64,128]{2,1,0:T(8,128)(2,1)S(1)}, u32[]{:S(2)}) copy-start(bf16[3,64,128]{2,1,0:T(8,128)(2,1)S(1)} %convolution_convert_fusion.8) | copy-start | bytes 147460
  139.5 29.5 %copy-start.52 = (f32[128,768]{1,0:T(8,128)}, f32[128,768]{1,0:T(8,128)S(1)}, u32[]{:S(2)}) copy-start(f32[128,768]{1,0:T(8,128)S(1)} %multiply_multiply_fusion) | copy-start | bytes 1179652
  141.9 27.4 %copy-start.115 = (f32[128]{0:T(128)}, f32[128]{0:T(128)S(1)}, u32[]{:S(2)}) copy-start(f32[128]{0:T(128)S(1)} %get-tuple-element.100) | copy-start | bytes 1540
  141.9 55.5 %copy-start.103 = (f32[128,4]{0,1:T(4,128)}, f32[128,4]{0,1:T(4,128)S(1)}, u32[]{:S(2)}) copy-start(f32[128,4]{0,1:T(4,128)S(1)} %get-tuple-element.101) | copy-start | bytes 6148
  143.7 25.3 %copy-start.62 = (bf16[2,128,768]{2,1,0:T(8,128)(2,1)S(1)}, bf16[2,128,768]{2,1,0:T(8,128)(2,1)}, u32[]{:S(2)}) copy-start(bf16[2,128,768]{2,1,0:T(8,128)(2,1)} %param.15) | copy-start | bytes 1179652
  169.3 28.1 %copy-start.131 = (f32[128]{0:T(128)}, f32[128]{0:T(128)S(1)}, u32[]{:S(2)}) copy-start(f32[128]{0:T(128)S(1)} %mul.403) | copy-start | bytes 1540
  169.7 27.7 %copy-start.6 = (bf16[4,32,768]{2,1,0:T(8,128)(2,1)S(1)}, bf16[4,32,768]{2,1,0:T(8,128)(2,1)}, u32[]{:S(2)}) copy-start(bf16[4,32,768]{2,1,0:T(8,128)(2,1)} %copy-done.5) | copy-start | bytes 589828
  169.7 27.8 %copy-start.37 = (bf16[128,768]{1,0:T(8,128)(2,1)S(1)}, bf16[128,768]{1,0:T(8,128)(2,1)}, u32[]{:S(2)}) copy-start(bf16[128,768]{1,0:T(8,128)(2,1)} %get-tuple-element.103) | copy-start | bytes 589828
  169.7 27.8 %copy-start.59 = (bf16[1,4,192,128]{3,2,1,0:T(8,128)(2,1)S(1)}, bf16[1,4,192,128]{3,2,1,0:T(8,128)(2,1)}, u32[]{:S(2)}) copy-start(bf16[1,4,192,128]{3,2,1,0:T(8,128)(2,1)} %get-tuple-element.120) | copy-start | bytes 589828
  169.7 27.8 %copy-start.109 = (s32[128]{0:T(128)S(1)}, s32[128]{0:T(128)}, u32[]{:S(2)}) copy-start(s32[128]{0:T(128)} %copy-done.108) | copy-start | bytes 1540
  169.7 27.8 %copy-start.123 = (f32[128]{0:T(128)S(1)}, f32[128]{0:T(128)}, u32[]{:S(2)}) copy-start(f32[128]{0:T(128)} %fusion.118) | copy-start | bytes 1540
  202.3 11.9 %copy-start.85 = (bf16[128,192]{1,0:T(8,128)(2,1)}, bf16[128,192]{1,0:T(8,128)(2,1)S(1)}, u32[]{:S(2)}) copy-start(bf16[128,192]{1,0:T(8,128)(2,1)S(1)} %copy.81) | copy-start | bytes 147460
  202.3 11.9 %copy-start.38 = (bf16[128,768]{1,0:T(8,128)(2,1)S(1)}, bf16[128,768]{1,0:T(8,128)(2,1)}, u32[]{:S(2)}) copy-start(bf16[128,768]{1,0:T(8,128)(2,1)} %get-tuple-element.103) | copy-start | bytes 589828
  202.3 11.9 %copy-start.124 = (f32[128]{0:T(128)S(1)}, f32[128]{0:T(128)}, u32[]{:S(2)}) copy-start(f32[128]{0:T(128)} %fusion.117) | copy-start | bytes 1540
  202.4 12.0 %copy-start.87 = (bf16[128,192]{1,0:T(8,128)(2,1)}, bf16[128,192]{1,0:T(8,128)(2,1)S(1)}, u32[]{:S(2)}) copy-start(bf16[128,192]{1,0:T(8,128)(2,1)S(1)} %copy.82) | copy-start | bytes 147460
  202.5 11.8 %copy-start.89 = (bf16[128,192]{1,0:T(8,128)(2,1)}, bf16[128,192]{1,0:T(8,128)(2,1)S(1)}, u32[]{:S(2)}) copy-start(bf16[128,192]{1,0:T(8,128)(2,1)S(1)} %copy.83) | copy-start | bytes 147460
  202.5 11.9 %copy-start.138 = (f32[128]{0:T(128)S(1)}, f32[128]{0:T(128)}, u32[]{:S(2)}) copy-start(f32[128]{0:T(128)} %copy-done.137) | copy-start | bytes 1540
  202.5 11.9 %copy-start.25 = (bf16[128,768]{1,0:T(8,128)(2,1)S(1)}, bf16[128,768]{1,0:T(8,128)(2,1)}, u32[]{:S(2)}) copy-start(bf16[128,768]{1,0:T(8,128)(2,1)} %copy-done.24) | copy-start | bytes 589828
  215.4 28.0 %copy-start.48 = (bf16[128,768]{1,0:T(8,128)(2,1)}, bf16[128,768]{1,0:T(8,128)(2,1)S(1)}, u32[]{:S(2)}) copy-start(bf16[128,768]{1,0:T(8,128)(2,1)S(1)} %get-tuple-element.99) | copy-start | bytes 589828
  215.6 26.5 %copy-start.133 = (f32[128]{0:T(128)}, f32[128]{0:T(128)S(1)}, u32[]{:S(2)}) copy-start(f32[128]{0:T(128)S(1)} %mul.424) | copy-start | bytes 1540
  215.7 26.4 %copy-start.4 = (bf16[4,32,768]{2,1,0:T(8,128)(2,1)S(1)}, bf16[4,32,768]{2,1,0:T(8,128)(2,1)}, u32[]{:S(2)}) copy-start(bf16[4,32,768]{2,1,0:T(8,128)(2,1)} %copy-done.2) | copy-start | bytes 589828
  215.7 26.4 %copy-start.46 = (bf16[2,128,768]{2,1,0:T(8,128)(2,1)S(1)}, bf16[2,128,768]{2,1,0:T(8,128)(2,1)}, u32[]{:S(2)}) copy-start(bf16[2,128,768]{2,1,0:T(8,128)(2,1)} %param.14) | copy-start | bytes 1179652
  215.7 26.4 %copy-start.57 = (bf16[1,4,192,128]{3,2,1,0:T(8,128)(2,1)S(1)}, bf16[1,4,192,128]{3,2,1,0:T(8,128)(2,1)}, u32[]{:S(2)}) copy-start(bf16[1,4,192,128]{3,2,1,0:T(8,128)(2,1)} %copy-done.56) | copy-start | bytes 589828
  215.7 26.4 %copy-start.101 = (f32[768]{0:T(1024)S(1)}, f32[768]{0:T(1024)}, u32[]{:S(2)}) copy-start(f32[768]{0:T(1024)} %copy-done.100) | copy-start | bytes 9220
  215.7 26.4 %copy-start.102 = (f32[128,4]{0,1:T(4,128)S(1)}, f32[128,4]{0,1:T(4,128)}, u32[]{:S(2)}) copy-start(f32[128,4]{0,1:T(4,128)} %get-tuple-element.105) | copy-start | bytes 6148
  215.7 26.4 %copy-start.106 = (s32[128]{0:T(128)S(1)}, s32[128]{0:T(128)}, u32[]{:S(2)}) copy-start(s32[128]{0:T(128)} %copy-done.105) | copy-start | bytes 1540
  215.7 26.4 %copy-start.122 = (f32[128]{0:T(128)S(1)}, f32[128]{0:T(128)}, u32[]{:S(2)}) copy-start(f32[128]{0:T(128)} %copy-done.121) | copy-start | bytes 1540
  245.9 12.4 %copy-start.91 = (bf16[128,192]{1,0:T(8,128)(2,1)}, bf16[128,192]{1,0:T(8,128)(2,1)S(1)}, u32[]{:S(2)}) copy-start(bf16[128,192]{1,0:T(8,128)(2,1)S(1)} %copy.87) | copy-start | bytes 147460
  245.9 12.4 %copy-start.47 = (bf16[2,128,768]{2,1,0:T(8,128)(2,1)S(1)}, bf16[2,128,768]{2,1,0:T(8,128)(2,1)}, u32[]{:S(2)}) copy-start(bf16[2,128,768]{2,1,0:T(8,128)(2,1)} %param.14) | copy-start | bytes 1179652
  245.9 12.4 %copy-start.113 = (f32[128]{0:T(128)S(1)}, f32[128]{0:T(128)}, u32[]{:S(2)}) copy-start(f32[128]{0:T(128)} %fusion.115) | copy-start | bytes 1540
  247.4 11.2 %copy-start.128 = (f32[128]{0:T(128)S(1)}, f32[128]{0:T(128)}, u32[]{:S(2)}) copy-start(f32[128]{0:T(128)} %copy-done.127) | copy-start | bytes 1540
  247.4 11.2 %copy-start.49 = (bf16[128,768]{1,0:T(8,128)(2,1)S(1)}, bf16[128,768]{1,0:T(8,128)(2,1)}, u32[]{:S(2)}) copy-start(bf16[128,768]{1,0:T(8,128)(2,1)} %copy-done.48) | copy-start | bytes 589828
  260.2 72.5 %collective-permute-start.1 = (bf16[128,768]{1,0:T(8,128)(2,1)}, bf16[128,768]{1,0:T(8,128)(2,1)}, u32[]{:S(2)}, u32[]{:S(2)}) collective-permute-start(bf16[128,768]{1,0:T(8,128)(2,1)} %broadcast_select_fusion.2), channel_id=1, source_target_pairs={{0,16},{16,0},{1,17},{17,1},{2,18},{18,2},{3,19},{19,3},{4,20},{20... | collective-permute-start | bytes 589832 | tf_op jit(solution)/shard_map/ppermute | solution.py:822
  261.2 73.3 %collective-permute-start = (bf16[128,768]{1,0:T(8,128)(2,1)}, bf16[128,768]{1,0:T(8,128)(2,1)}, u32[]{:S(2)}, u32[]{:S(2)}) collective-permute-start(bf16[128,768]{1,0:T(8,128)(2,1)} %get-tuple-element.113), channel_id=1, source_target_pairs={{0,16},{16,0},{1,17},{17,1},{2,18},{18,2},{3,19},{19,3},{4,20},{20... | collective-permute-start | bytes 589832 | tf_op jit(solution)/shard_map/ppermute | solution.py:822
  261.9 6.3 %copy-start.125 = (s32[4,8]{1,0:T(4,128)}, s32[4,8]{1,0:T(4,128)S(1)}, u32[]{:S(2)}) copy-start(s32[4,8]{1,0:T(4,128)S(1)} %multiply_add_fusion) | copy-start | bytes 388
  288.4 36.5 %copy-start.13 = (bf16[768,768]{1,0:T(8,128)(2,1)S(1)}, bf16[768,768]{1,0:T(8,128)(2,1)}, u32[]{:S(2)}) copy-start(bf16[768,768]{1,0:T(8,128)(2,1)} %copy-done.12) | copy-start | bytes 3538948
  (95 other events, 198.6 us)
